TPU v7x, 32 devices: a whole 2x2x4 slice. The times are simulated.
32 devices in a mesh: section: 2 (over core), expert: 4 (over y, x), shard: 4 (over z).
Axes of the slice: x: 2, y: 2, z: 4, core: 2. Of those that a mesh axis runs over, the one named last changes fastest.
Arguments:
- feed: bfloat16 [2, 2, 1024, 768], P('section', None, ('expert', 'shard')), may hold values from -6 to 6
- segments: int32 [2, 16, 64], P(None, ('expert', 'shard')), may hold values from 0 to 3, never falling along the last dimension, each value on 1 to 32 neighbouring positions
- routes: int32 [2, 2, 16, 64], P('section', None, ('expert', 'shard')), may hold values from 0 to 3, as said below
- rel_bucket: int32 [127], replicated, may hold values from 0 to 31
- gain_attn: bfloat16 [2, 768], P('section', ('expert', 'shard')), may hold values from 0.099609375 to 1.8984375
- gain_ffn: bfloat16 [2, 768], P('section', ('expert', 'shard')), may hold values from 0.099609375 to 1.8984375
- w_query: bfloat16 [2, 768, 768], P('section', ('expert', 'shard')), may hold values from -0.21875 to 0.21875
- w_key: bfloat16 [2, 768, 768], P('section', ('expert', 'shard')), may hold values from -0.21875 to 0.21875
- w_value: bfloat16 [2, 768, 768], P('section', ('expert', 'shard')), may hold values from -0.21875 to 0.21875
- w_out_attn: bfloat16 [2, 768, 768], P('section', ('expert', 'shard')), may hold values from -0.875 to 0.875
- rel_table: bfloat16 [2, 384], P('section', ('expert', 'shard')), may hold values from -4 to 4
- router: bfloat16 [2, 768, 4], P('section', ('expert', 'shard')), may hold values from -0.15625 to 0.15625
- expert_in: bfloat16 [2, 4, 768, 3072], P('section', 'expert', None, 'shard'), may hold values from -0.21875 to 0.21875
- expert_out: bfloat16 [2, 4, 3072, 768], P('section', 'expert', 'shard'), may hold values from -0.4375 to 0.4375
Outputs:
- layer_out: bfloat16 [2, 2, 1024, 768], P('section', None, ('expert', 'shard'))
- layer_in_grad: bfloat16 [2, 2, 1024, 768], P('section', None, ('expert', 'shard'))
- grad_gain_attn: float32 [2, 768], P('section', ('expert', 'shard'))
- grad_gain_ffn: float32 [2, 768], P('section', ('expert', 'shard'))
- grad_w_query: float32 [2, 768, 768], P('section', ('expert', 'shard'))
- grad_w_key: float32 [2, 768, 768], P('section', ('expert', 'shard'))
- grad_w_value: float32 [2, 768, 768], P('section', ('expert', 'shard'))
- grad_w_out_attn: float32 [2, 768, 768], P('section', ('expert', 'shard'))
- grad_rel_table: float32 [2, 384], P('section', ('expert', 'shard'))
- grad_router: float32 [2, 768, 4], P('section', ('expert', 'shard'))
- grad_expert_in: float32 [2, 4, 768, 3072], P('section', 'expert', None, 'shard')
- grad_expert_out: float32 [2, 4, 3072, 768], P('section', 'expert', 'shard')
Inputs may be any that keep to these rules, and one draw needn't show every extreme that they name: `routes`: in each micro-batch of each layer no expert is named by more than 32 tokens of one sequence, and one expert, drawn from the seed, is named by exactly 32 tokens of every sequence. `segments`: along each sequence the segment numbers never fall.
All inputs are finite; a program needn't handle non-finite values.
Results may differ from a plain program's by a relative error of at most 0.022.
Values may be sent and summed in bfloat16 or wider, within the bound.
No kernel may reach another device: no remote copies, remote signals or barrier semaphores. Data moves between devices by JAX's collectives and lax.ppermute only.
A program may use at most 128 MiB of HBM per device.

v0:
```python
import functools
import math

import jax
import jax.numpy as jnp
import numpy as np
from jax import lax
from jax.experimental import pallas as pl
from jax.experimental.pallas import tpu as pltpu
from jax.sharding import PartitionSpec as P

HEADS = 12
HEAD_DIM = 64
NB = 32
EXT = 128
LEAD = 3
EPSILON = 1e-06
MASK_FILL = -1e30
BF = jnp.bfloat16
F32 = jnp.float32
VM = pl.BlockSpec()
SM = pl.BlockSpec(memory_space=pltpu.SMEM)
HB = pl.BlockSpec(memory_space=pltpu.HBM)
AN = pl.BlockSpec(memory_space=pl.ANY)


def dot(a, b):
    return jnp.dot(a, b, preferred_element_type=F32)


def dot_t(a, b):
    return lax.dot_general(a, b, (((1,), (1,)), ((), ())), preferred_element_type=F32)


def t_dot(a, b):
    return lax.dot_general(a, b, (((0,), (0,)), ((), ())), preferred_element_type=F32)


def swap(value):
    return lax.ppermute(value, "section", [(0, 1), (1, 0)])


def direct(axis):
    count = lax.axis_size(axis)
    return count <= 4 and count & (count - 1) == 0


def peer_ids(axis):
    count = lax.axis_size(axis)
    ids = jnp.arange(count, dtype=jnp.int32)
    return ids ^ lax.axis_index(axis) if direct(axis) else ids


def hop(value, axis, step):
    count = lax.axis_size(axis)
    return lax.ppermute(value, axis, [(i, i ^ step) for i in range(count)])


def spread(value, axis):
    count = lax.axis_size(axis)
    if direct(axis):
        return [value] + [hop(value, axis, step) for step in range(1, count)]
    every = lax.all_gather(value, axis, axis=0)
    return [every[i] for i in range(count)]


def exchange(blocks, axis):
    count = lax.axis_size(axis)
    if direct(axis):
        return [blocks[0]] + [hop(blocks[step], axis, step) for step in range(1, count)]
    swapped = lax.all_to_all(jnp.stack(blocks), axis, 0, 0, tiled=True)
    return [swapped[i] for i in range(count)]


def scatter_rows(whole):
    for axis in ("expert", "shard"):
        count = lax.axis_size(axis)
        rows = whole.shape[0] // count
        ids = peer_ids(axis)
        blocks = [
            lax.dynamic_slice_in_dim(whole, ids[i] * rows, rows, axis=0).astype(BF)
            for i in range(count)
        ]
        whole = sum(block.astype(F32) for block in exchange(blocks, axis))
    return whole


def call(kernel, outs, ins, specs, scratch=(), flops=0, out_specs=None, after=(), limit=28):
    count = len(ins)
    moved = sum(math.prod(a.shape) * a.dtype.itemsize for a in (*ins, *outs))

    def run(*refs):
        kernel(*refs[:count], *refs[count + len(after) :])

    return pl.pallas_call(
        run,
        out_shape=list(outs),
        in_specs=list(specs) + [AN] * len(after),
        out_specs=list(out_specs or [VM] * len(outs)),
        scratch_shapes=list(scratch),
        compiler_params=pltpu.CompilerParams(vmem_limit_bytes=limit * 1024 * 1024),
        cost_estimate=pl.CostEstimate(flops=flops, bytes_accessed=moved, transcendentals=0),
    )(*ins, *after)


def out(shape, kind=BF):
    return jax.ShapeDtypeStruct(shape, kind)


def begin(copies):
    for copy in copies:
        copy.start()
    return copies


def finish(copies):
    for copy in copies:
        copy.wait()


def join_weights(place, pieces, held, layout):
    plane = pieces[0].shape[0]
    for part in range(2):
        target = place[0] if part == 0 else 1 - place[0]
        for i, (peer, first) in enumerate(layout):
            piece = pieces[part * len(layout) + i]
            at = pl.multiple_of(place[2 + peer] * plane + first, piece.shape[0])
            held[target, pl.ds(at, piece.shape[0]), :] = piece[...]


def as_column(row, turned=None):
    n = row.shape[1]
    across = lax.broadcasted_iota(jnp.int32, (n, n), 1)
    down = lax.broadcasted_iota(jnp.int32, (n, n), 0)
    if turned is not None:
        down = turned - down
    return jnp.sum(jnp.where(across == down, row, jnp.zeros_like(row)), axis=1, keepdims=True)


def table_places(width, own_rows, table_rows):
    spot = lax.broadcasted_iota(jnp.int32, (16, width), 1).astype(F32)
    owner = jnp.floor((spot + 0.5) * (1.0 / own_rows))
    rest = spot - owner * own_rows
    flat = owner * table_rows + rest
    bucket = jnp.floor((flat + 0.5) * (1.0 / HEADS))
    head = flat - bucket * HEADS
    real = rest < table_rows
    row = lax.broadcasted_iota(jnp.int32, (16, width), 0).astype(F32)
    return jnp.where(real, bucket, -1.0)[0:1], (real & (head == row)).astype(F32)


def inverse_rms(value):
    return lax.rsqrt(jnp.mean(value * value, axis=-1, keepdims=True) + EPSILON)


def norm_back(value, gain, grad):
    scale = inverse_rms(value)
    scaled = value * scale
    gained = grad * gain
    back = scale * (gained - scaled * jnp.mean(gained * scaled, axis=-1, keepdims=True))
    return back, jnp.sum(grad * scaled, axis=0, keepdims=True)


def gain_rows(side):
    pick = (
        lax.broadcasted_iota(jnp.int32, (16, EXT), 0)
        == lax.broadcasted_iota(jnp.int32, (16, EXT), 1)
    ).astype(BF)
    rows = dot_t(pick, side)
    return rows[0:1], rows[1:2], rows[2:3]


def gelu_parts(value):
    c = math.sqrt(2.0 / math.pi)
    square = value * value
    inner = jnp.tanh(c * (value + 0.044715 * square * value))
    grad = 0.5 * (1.0 + inner) + 0.5 * value * (1.0 - inner * inner) * (
        c + (3.0 * 0.044715 * c) * square
    )
    return 0.5 * value * (1.0 + inner), grad


def softmax_lanes(logits, experts):
    lane = lax.broadcasted_iota(jnp.int32, logits.shape, 1)
    valid = (lane >= LEAD) & (lane < LEAD + experts)
    logits = jnp.where(valid, logits, MASK_FILL)
    power = jnp.exp(logits - jnp.max(logits, axis=-1, keepdims=True))
    power = jnp.where(valid, power, 0.0)
    return power / jnp.sum(power, axis=-1, keepdims=True), lane


def pair_rows(value):
    low_lanes = lax.broadcasted_iota(jnp.int32, value.shape, 1) < HEAD_DIM
    zero = jnp.zeros_like(value)
    return jnp.concatenate(
        [jnp.where(low_lanes, value, zero), jnp.where(low_lanes, zero, value)], axis=0
    )


def pair_lanes(value):
    half = value.shape[0] // 2
    low_lanes = lax.broadcasted_iota(jnp.int32, (half, value.shape[1]), 1) < HEAD_DIM
    return jnp.where(low_lanes, value[:half], value[half:])


def attn_forward(layer, seq, width, experts, layout, count, shards, own_rows, table_rows, *refs):
    place, info = refs[:2]
    refs = refs[2:]
    pieces, refs = refs[:count], refs[count:]
    if layer == 0:
        (x_ref,), refs = refs[:1], refs[1:]
        n2_ref, refs = refs[0], refs[1:]
        extra = []
    else:
        (hid_ref,), toks, refs = refs[:1], refs[1:-16], refs[-16:]
        out_ref, n2_ref, tok_out = refs[:3]
        refs = refs[3:]
    acts_out, probs_out, floats_out, ext_out, held_out = refs[:5]
    held, sem, acts, probs_keep, floats, ext_keep, low_keep, out_sems = refs[5:]
    if layer == 0:
        low = x_ref[...]
    else:
        coming = pltpu.make_async_copy(hid_ref, floats, out_sems.at[0])
        coming.start()
        tok = sum(t[...].astype(F32) for t in toks).astype(BF)
        low_keep[...] = tok
        coming.wait()
        gate = floats[:, width + EXT : width + EXT + 1]
        low = (floats[:, :width] + gate * tok.astype(F32)).astype(BF)
        out_ref[...] = low
        extra = begin([pltpu.make_async_copy(low_keep, tok_out, out_sems.at[0])])
    acts[:, 6 * width :] = low
    x = low.astype(F32)
    scaled = x * inverse_rms(x)
    seg_row = info[0:1, :seq]
    same = as_column(seg_row) == seg_row
    route = as_column(info[1 + layer : 2 + layer, :seq])
    bucket = as_column(info[3:4, :]).astype(F32)
    bucket_row, head_sel = table_places(width, own_rows, table_rows)
    buckets = (bucket == bucket_row).astype(BF)
    if layout:
        join_weights(place, pieces, held, layout)
    else:
        held[place[0]] = pieces[0][...]
        held[1 - place[0]] = pieces[1][...]
    extra = extra + begin([pltpu.make_async_copy(held, held_out, sem)])
    side = held[0, :, 2 * width : 2 * width + EXT]
    ext_keep[...] = side
    extra = extra + begin([pltpu.make_async_copy(ext_keep, ext_out, out_sems.at[1])])
    gain_one, gain_two, table_row = gain_rows(side)
    table = dot_t((head_sel * table_row).astype(BF), buckets)
    normed = (scaled * gain_one).astype(BF)
    acts[:, :width] = normed
    acts[:, width : 3 * width] = dot(normed, held[0, :, : 2 * width]).astype(BF)
    acts[:, 3 * width : 4 * width] = dot(normed, held[1, :, :width]).astype(BF)
    scale = 1.0 / math.sqrt(HEAD_DIM)
    contexts = []
    for p in range(HEADS // 2):
        at = [(1 + i) * width + 128 * p for i in range(3)]
        q2 = pair_rows(acts[:, at[0] : at[0] + 128])
        scores = dot_t(q2, acts[:, at[1] : at[1] + 128]) * scale
        parts = []
        for h in (2 * p, 2 * p + 1):
            line = jnp.broadcast_to(table[h : h + 1], (seq, 2 * seq))
            bias = pltpu.roll(line, seq + 1, axis=1, stride=1, stride_axis=0)[:, :seq]
            part = scores[seq * (h - 2 * p) : seq * (h - 2 * p) + seq] + bias
            parts.append(jnp.where(same, part, MASK_FILL))
        scores = jnp.concatenate(parts, axis=0)
        power = jnp.exp(scores - jnp.max(scores, axis=-1, keepdims=True))
        probs = power / jnp.sum(power, axis=-1, keepdims=True)
        probs_keep[p] = probs
        contexts.append(pair_lanes(dot(probs.astype(BF), acts[:, at[2] : at[2] + 128])))
    extra = extra + begin([pltpu.make_async_copy(probs_keep, probs_out, out_sems.at[2])])
    context = jnp.concatenate(contexts, axis=1).astype(BF)
    acts[:, 4 * width : 5 * width] = context
    hidden = x + dot(context, held[1, :, width : 2 * width])
    floats[:, :width] = hidden
    normed_two = (hidden * inverse_rms(hidden) * gain_two).astype(BF)
    n2_ref[...] = normed_two
    acts[:, 5 * width : 6 * width] = normed_two
    extra = extra + begin([pltpu.make_async_copy(acts, acts_out, out_sems.at[3])])
    gates, lane = softmax_lanes(dot(normed_two, side), experts)
    floats[:, width : width + EXT] = gates
    value = jnp.sum(jnp.where(lane == route + LEAD, gates, 0.0), axis=-1, keepdims=True)
    floats[:, width + EXT :] = jnp.broadcast_to(value, gates.shape)
    finish(extra + begin([pltpu.make_async_copy(floats, floats_out, out_sems.at[4])]))


def pick_inputs(seq, *refs):
    place, own_feed, came_feed, segments, own_routes, came_routes, buckets = refs[:7]
    x_ref, dy_ref, info, sems = refs[7:]
    sec = place[0]
    for core in range(2):

        @pl.when(sec == core)
        def _(core=core):
            sources = (own_feed, came_feed) if core == 0 else (came_feed, own_feed)
            finish(
                begin(
                    [
                        pltpu.make_async_copy(sources[0].at[core], x_ref, sems.at[0]),
                        pltpu.make_async_copy(sources[1].at[core], dy_ref, sems.at[1]),
                    ]
                )
            )
            info[...] = jnp.full(info.shape, -2, jnp.int32)
            info[0:1, :seq] = segments[core : core + 1, :]
            info[1 + core : 2 + core, :seq] = own_routes[core : core + 1, :]
            info[2 - core : 3 - core, :seq] = came_routes[core : core + 1, :]
            info[3:4, : 2 * seq - 1] = buckets[...]


def routing_slots(shards, seq, experts, cap, *refs):
    place, infos, slots = refs[0], refs[1 : 1 + shards], refs[1 + shards]
    before = (
        lax.broadcasted_iota(jnp.int32, (seq, seq), 0)
        < lax.broadcasted_iota(jnp.int32, (seq, seq), 1)
    ).astype(BF)
    routes = jnp.concatenate(
        [info[1 + layer : 2 + layer, :seq] for layer in range(2) for info in infos], axis=0
    )
    rank = jnp.zeros(routes.shape, F32)
    for e in range(experts):
        mine = (routes == e).astype(F32)
        rank = rank + mine * dot(mine.astype(BF), before)
    slots[...] = (routes ^ place[1]) * cap + rank.astype(jnp.int32)


def slot_hot(slots, layer, shards, z, total):
    row = slots[layer * shards + z : layer * shards + z + 1, :]
    return (lax.broadcasted_iota(jnp.int32, (total, row.shape[1]), 0) == row).astype(BF)


def dispatch_rows(layer, count, shards, cap, *refs):
    slots = refs[0]
    toks = refs[1 : 1 + shards]
    blocks = refs[1 + shards :]
    for z in range(shards):
        rows = dot(slot_hot(slots, layer, shards, z, count * cap), toks[z][...]).astype(BF)
        for i in range(count):
            blocks[i][z * cap : (z + 1) * cap, :] = rows[i * cap : (i + 1) * cap]


def combine_rows(layer, count, shards, cap, *refs):
    slots = refs[0]
    blocks, refs = refs[1 : 1 + count], refs[1 + count :]
    more = (len(refs) - shards) // 2
    handed, toks, given = refs[:more], refs[more : more + shards], refs[more + shards :]
    for z in range(shards):
        rows = jnp.concatenate([b[z * cap : (z + 1) * cap, :] for b in blocks], axis=0)
        toks[z][...] = t_dot(slot_hot(slots, layer, shards, z, count * cap), rows).astype(BF)
    for source, target in zip(handed, given):
        target[...] = source[...]


def start_expert(layer, place, own, came, held, sems):
    def begin(pair):
        for i in range(2):
            pltpu.make_async_copy(pair[i], held.at[i], sems.at[i]).start()

    @pl.when(place[0] == layer)
    def _():
        begin(own)

    @pl.when(place[0] != layer)
    def _():
        begin(came)

    return [pltpu.make_async_copy(own[i], held.at[i], sems.at[i]) for i in range(2)]


def expert_forward(layer, count, *refs):
    place, own, came = refs[0], refs[1:3], refs[3:5]
    blocks = refs[5 : 5 + count]
    results, rows_out = refs[5 + count : 5 + 2 * count], refs[5 + 2 * count]
    held, sems, rows, out_sem = refs[6 + 2 * count :]
    copies = start_expert(layer, place, own, came, held, sems)
    each = blocks[0].shape[0]
    for i in range(count):
        rows[i * each : (i + 1) * each, :] = blocks[i][...]
    leaving = begin([pltpu.make_async_copy(rows, rows_out, out_sem)])
    finish(copies)
    for i in range(count):
        activated = gelu_parts(dot(blocks[i][...], held[0]))[0].astype(BF)
        results[i][...] = dot(activated, held[1]).astype(BF)
    finish(leaving)


def expert_backward(layer, count, experts, with_out, *refs):
    place, own, came, ext_in = refs[0], refs[1:3], refs[3:5], refs[5]
    if with_out:
        blocks, dy_in, refs = refs[6 : 6 + count], refs[6 + count : 6 + 2 * count], refs[6 + 2 * count :]
    else:
        rows_in, dys, refs = refs[6], refs[7 : 7 + count], refs[7 + count :]
    grads, refs = refs[:count], refs[count:]
    if with_out:
        results, refs = refs[:count], refs[count:]
    keep_out, held, sems, keep, ext, late, more_sems = refs
    copies = start_expert(layer, place, own, came, held, sems)
    each = grads[0].shape[0]
    loads = [pltpu.make_async_copy(ext_in, ext, more_sems.at[0])]
    if with_out:
        loads += [
            pltpu.make_async_copy(dy_in[i], late.at[pl.ds(i * each, each), :], more_sems.at[1 + i])
            for i in range(count)
        ]
    else:
        loads += [pltpu.make_async_copy(rows_in, late, more_sems.at[1])]
    begin(loads)
    finish(loads + copies)
    leaving = []
    for i in range(count):
        at = slice(i * each, (i + 1) * each)
        if with_out:
            rows, dy = blocks[i][...], late[at, :]
        else:
            rows, dy = late[at, :], dys[i][...]
        dy = dy.astype(F32)
        gates, lane = softmax_lanes(dot(rows, ext[...]), experts)
        mine = (lane == place[1] + LEAD).astype(F32)
        value = jnp.sum(gates * mine, axis=-1, keepdims=True)
        grad_expert = (value * dy).astype(BF)
        act, slope = gelu_parts(dot(rows, held[0]))
        act = act.astype(BF)
        grad_pre = (dot_t(grad_expert, held[1]) * slope).astype(BF)
        grad = dot_t(grad_pre, held[0])
        if with_out:
            result = dot(act, held[1])
            results[i][...] = result.astype(BF)
            grad_gate = jnp.sum(dy * result, axis=-1, keepdims=True)
            grad_logits = (grad_gate * value * (mine - gates)).astype(BF)
            grad = grad + dot_t(grad_logits, ext[...])
        grads[i][...] = grad.astype(BF)
        keep[0, at, :] = rows
        keep[1, at, :] = grad_pre
        keep[2, at, :] = act
        keep[3, at, :] = grad_expert
        leaving += begin(
            [
                pltpu.make_async_copy(
                    keep.at[:, pl.ds(i * each, each), :],
                    keep_out.at[:, pl.ds(i * each, each), :],
                    more_sems.at[1 + count + i],
                )
            ]
        )
    finish(leaving)


def attn_backward(layer, seq, width, experts, shards, own_rows, table_rows, *refs):
    place, info, held_in = refs[:3]
    refs = refs[3:]
    dy_ref, acts_in, probs_in, floats_in = refs[:4]
    refs = refs[4:]
    if layer == 0:
        tok_in, refs = refs[0], refs[1:]
    parts, refs = refs[:shards], refs[shards:]
    dx_ref, ship, stay, side_grad = refs[:4]
    ship_all, ship = ship, ship.at[pl.ds(0, seq), :]
    held, sem, acts, probs_all, floats, tok_keep, gj, g_rel, in_sems = refs[4:]
    loads = [
        pltpu.make_async_copy(floats_in, floats, in_sems.at[0]),
        pltpu.make_async_copy(acts_in, acts, in_sems.at[1]),
        pltpu.make_async_copy(probs_in, probs_all, in_sems.at[2]),
    ]
    if layer == 0:
        loads.append(pltpu.make_async_copy(tok_in, tok_keep, in_sems.at[3]))
    begin(loads)
    copies = begin([pltpu.make_async_copy(held_in, held, sem)])
    dy = dy_ref[...].astype(F32)
    grad_norm_two = sum(p[...].astype(F32) for p in parts)
    route = as_column(info[1 + layer : 2 + layer, :seq])
    bucket = as_column(info[3:4, :], 2 * seq - 2).astype(F32)
    bucket_row, head_sel = table_places(width, own_rows, table_rows)
    buckets = (bucket == bucket_row).astype(BF)
    finish(loads)
    hidden = floats[:, :width]
    x = acts[:, 6 * width :].astype(F32)
    state = acts
    finish(copies)
    side = held[0, :, 2 * width : 2 * width + EXT]
    gain_one, gain_two, _ = gain_rows(side)
    side_grad[...] = jnp.zeros_like(side_grad)
    if layer == 0:
        gates = floats[:, width : width + EXT]
        lane = lax.broadcasted_iota(jnp.int32, gates.shape, 1)
        hot = (lane == route + LEAD).astype(F32)
        grad_gate = jnp.sum(dy * tok_keep[...].astype(F32), axis=-1, keepdims=True)
        value = floats[:, width + EXT : width + EXT + 1]
        grad_logits = (grad_gate * value * (hot - gates)).astype(BF)
        grad_norm_two = grad_norm_two + dot_t(grad_logits, side)
        router_rows = t_dot(grad_logits, acts[:, 5 * width : 6 * width])
        side_grad[...] = router_rows[: side_grad.shape[0]]
    back, gain_two_grad = norm_back(hidden, gain_two, grad_norm_two)
    grad_hidden = dy + back
    grad_hidden_low = grad_hidden.astype(BF)
    grad_context = dot_t(grad_hidden_low, held[1, :, width : 2 * width]).astype(BF)
    scale = 1.0 / math.sqrt(HEAD_DIM)
    mirror = (
        lax.broadcasted_iota(jnp.int32, (seq, 2 * seq), 0)
        + lax.broadcasted_iota(jnp.int32, (seq, 2 * seq), 1)
        == seq - 1
    ).astype(BF)
    for p in range(HEADS // 2):
        lanes = slice(128 * p, 128 * p + 128)
        q2 = pair_rows(state[:, width + 128 * p : width + 128 * p + 128])
        keys = state[:, 2 * width + 128 * p : 2 * width + 128 * p + 128]
        vals = state[:, 3 * width + 128 * p : 3 * width + 128 * p + 128]
        g2 = pair_rows(grad_context[:, lanes])
        probs = probs_all[p]
        grad_probs = dot_t(g2, vals)
        grad_scores = probs * (
            grad_probs - jnp.sum(probs * grad_probs, axis=-1, keepdims=True)
        )
        grad_scores = grad_scores.astype(BF)
        gj[:, lanes] = (pair_lanes(dot(grad_scores, keys)) * scale).astype(BF)
        gj[:, width + 128 * p : width + 128 * p + 128] = (t_dot(grad_scores, q2) * scale).astype(BF)
        gj[:, 2 * width + 128 * p : 2 * width + 128 * p + 128] = t_dot(
            probs.astype(BF), g2
        ).astype(BF)
        turned = dot(grad_scores, mirror)
        for h in range(2):
            shifted = pltpu.roll(turned[h * seq : (h + 1) * seq], 0, axis=1, stride=1, stride_axis=0)
            g_rel[2 * p + h : 2 * p + h + 1, :] = jnp.sum(shifted, axis=0, keepdims=True)
    g_rel[HEADS:, :] = jnp.zeros_like(g_rel[HEADS:, :])
    offsets = g_rel[...]
    high = offsets.astype(BF)
    low = (offsets - high.astype(F32)).astype(BF)
    by_row = dot(high, buckets) + dot(low, buckets)
    side_grad[2:3, :] = jnp.sum(by_row * head_sel, axis=0, keepdims=True)
    side_grad[1:2, :] = gain_two_grad
    grad_normed = dot_t(gj[:, : 2 * width], held[0, :, : 2 * width]) + dot_t(
        gj[:, 2 * width :], held[1, :, :width]
    )
    back, gain_one_grad = norm_back(x, gain_one, grad_normed)
    side_grad[0:1, :] = gain_one_grad
    dx_ref[...] = (grad_hidden + back).astype(BF)
    normed = state[:, :width]
    halves = (ship, stay)
    for core in range(2):

        @pl.when(place[0] == core)
        def _(core=core):
            halves[1 - core][:, :width] = normed
            halves[1 - core][:, width : 3 * width] = gj[:, : 2 * width]
            halves[1 - core][:, 3 * width :] = jnp.zeros_like(normed)
            halves[core][:, :width] = normed
            halves[core][:, width : 2 * width] = gj[:, 2 * width :]
            halves[core][:, 2 * width : 3 * width] = state[:, 4 * width : 5 * width]
            halves[core][:, 3 * width :] = grad_hidden_low

    ship_all[seq:, :width] = side_grad[...].astype(BF)
    ship_all[seq:, width:] = jnp.zeros_like(ship_all[seq:, width:])


def last_output(seq, width, experts, shards, *refs):
    info, dy_ref, acts_in, floats_in, side_in = refs[:5]
    parts, refs = refs[5 : 5 + shards], refs[5 + shards :]
    out_ref, side_grad, normed, floats, sems = refs
    loads = begin(
        [
            pltpu.make_async_copy(floats_in, floats, sems.at[0]),
            pltpu.make_async_copy(acts_in.at[:, pl.ds(5 * width, width)], normed, sems.at[1]),
        ]
    )
    tok = sum(p[...].astype(F32) for p in parts).astype(BF).astype(F32)
    finish(loads)
    value = floats[:, width + EXT : width + EXT + 1]
    out_ref[...] = (floats[:, :width] + value * tok).astype(BF)
    gates = floats[:, width : width + EXT]
    lane = lax.broadcasted_iota(jnp.int32, gates.shape, 1)
    hot = (lane == as_column(info[2:3, :seq]) + LEAD).astype(F32)
    grad_gate = jnp.sum(dy_ref[...].astype(F32) * tok, axis=-1, keepdims=True)
    grad_logits = (grad_gate * value * (hot - gates)).astype(BF)
    side_grad[...] = side_in[...] + t_dot(grad_logits, normed[...])[: side_grad.shape[0]]


def attn_weights(width, count, parts, more, relay, *refs):
    place, stay, came = refs[:3]
    total = refs[-1]
    handed, sides, outs = refs[3 : 3 + more], refs[3 + more : -1 - count - more], refs[-1 - count - more : -1]
    blocks, given = outs[:count], outs[count:]
    for source, target in zip(handed, given):
        target[...] = source[...]

    seq = stay.shape[0]

    def both(first, last):
        return jnp.concatenate([stay[:, first:last], came[:seq, first:last]], axis=0)

    unit = width // 2
    for i, part in enumerate(parts):
        at = slice(i * unit, (i + 1) * unit)

        @pl.when(place[0] == 0)
        def _(part=part, at=at):
            total[:, at] = t_dot(
                both(0, width), both(width + part * unit, width + (part + 1) * unit)
            ).astype(BF)

        @pl.when(place[0] != 0)
        def _(part=part, at=at):
            left = part // 2 * 2 * width
            right = left + width + part % 2 * unit
            total[:, at] = t_dot(both(left, left + width), both(right, right + unit)).astype(BF)

    if sides:
        block = jnp.zeros((width, EXT), F32)
        ours = (sides[0][...] + came[seq:, :width].astype(F32), sides[1][...] + sides[2][...])
        for layer, rows in enumerate(ours):
            pick = (
                lax.broadcasted_iota(jnp.int32, (rows.shape[0], EXT), 0) + layer * (EXT // 2)
                == lax.broadcasted_iota(jnp.int32, (rows.shape[0], EXT), 1)
            ).astype(BF)
            block = block + t_dot(rows.astype(BF), pick)
        total[:, len(parts) * unit :] = block.astype(BF)

    if relay:
        rows = blocks[0].shape[0] // 2
        cut = blocks[0].shape[1]
        columns = (slice(0, cut), slice(cut, total.shape[1]))
        for block, ids, at in zip(blocks, ((1, 3), (0, 2), (2, 3), (0, 1)), (0, 0, 1, 1)):
            for i, peer in enumerate(ids):
                first = pl.multiple_of(place[2 + peer] * rows, rows)
                block[i * rows : (i + 1) * rows, :] = total[pl.ds(first, rows), columns[at]]
        return
    rows = blocks[0].shape[0]
    for i in range(count):
        first = pl.multiple_of(place[2 + i] * rows, rows) if count > 1 else 0
        blocks[i][...] = total[pl.ds(first, rows), :]


def halve_sums(*refs):
    came_x, kept_x, came_y, kept_y, own_x, on_x, own_y, on_y = refs
    for came, kept, own, on in ((came_x, kept_x, own_x, on_x), (came_y, kept_y, own_y, on_y)):
        rows = own.shape[0]
        own[...] = came[:rows].astype(F32) + kept[:rows].astype(F32)
        on[...] = (came[rows:].astype(F32) + kept[rows:].astype(F32)).astype(BF)


def join_sums(at, *refs):
    place, own_x, came_x, own_y, came_y = refs[:5]
    blocks, total = refs[5:-1], refs[-1]
    cut = own_x.shape[1]
    total[:, :cut] = own_x[...] + came_x[...].astype(F32)
    total[:, cut:] = own_y[...] + came_y[...].astype(F32)
    rows = blocks[0].shape[0]
    for i, block in enumerate(blocks):
        first = pl.multiple_of(place[at + i] * rows, rows)
        block[...] = total[pl.ds(first, rows), :].astype(block.dtype)


def last_swap(width, *refs):
    place, zero, one, send = refs

    @pl.when(place[0] == 0)
    def _():
        send[:, : 2 * width] = one[...]
        send[:, 2 * width :] = zero[:, 2 * width :]

    @pl.when(place[0] != 0)
    def _():
        send[...] = zero[...]


def last_grads(width, experts, *refs):
    place, zero, one, came = refs[:4]
    query, key, value, out_proj, gain_a, gain_f, table, router = refs[4:]

    def put_side(side):
        n = side.shape[0]
        across = lax.broadcasted_iota(jnp.int32, (n, n), 1)
        down = lax.broadcasted_iota(jnp.int32, (n, n), 0)

        def turned(i):
            return jnp.sum(
                jnp.where(across == down, side[:, i : i + 1], 0.0), axis=0, keepdims=True
            )

        for i, target in enumerate((gain_a, gain_f, table)):
            target[...] = turned(i)[:, : target.shape[1]]
        for e in range(experts):
            router[e : e + 1, :] = turned(LEAD + e)

    @pl.when(place[0] == 0)
    def _():
        query[...] = zero[:, :width]
        key[...] = zero[:, width : 2 * width]
        value[...] = came[:, :width]
        out_proj[...] = came[:, width : 2 * width]
        put_side(zero[:, 2 * width : 2 * width + EXT // 2])

    @pl.when(place[0] != 0)
    def _():
        query[...] = came[:, :width]
        key[...] = came[:, width : 2 * width]
        value[...] = one[:, :width]
        out_proj[...] = one[:, width:]
        put_side(came[:, 2 * width + EXT // 2 :])


def sum_blocks(count, at, *refs):
    place, parts = refs[0], refs[1 : 1 + count]
    blocks, total = refs[1 + count : -1], refs[-1]
    total[...] = sum(p[...].astype(F32) for p in parts)
    rows = blocks[0].shape[0]
    for i, block in enumerate(blocks):
        first = pl.multiple_of(place[at + i] * rows, rows) if len(blocks) > 1 else 0
        block[...] = total[pl.ds(first, rows), :].astype(block.dtype)


def join_rows(count, first_id, *refs):
    place, parts, whole = refs[0], refs[1 : 1 + count], refs[1 + count]
    rows = parts[0].shape[0]
    for i in range(count):
        at = pl.multiple_of(place[first_id + i] * rows, rows)
        whole[pl.ds(at, rows), :] = parts[i][...]


def pick_later(*refs):
    place, kept, came, later = refs

    @pl.when(place[0] == 0)
    def _():
        later[...] = came[...]

    @pl.when(place[0] != 0)
    def _():
        later[...] = kept[...]


def join_planes(layout, *refs):
    place, pieces, whole = refs[0], refs[1:-1], refs[-1]
    plane = pieces[0].shape[0]
    for (peer, first), piece in zip(layout, pieces):
        at = pl.multiple_of(place[2 + peer] * plane + first, piece.shape[0])
        whole[pl.ds(at, piece.shape[0]), :] = piece[...]


def pack_weights(width, experts, table_rows, *refs):
    place, query, key, value, out_proj, gain_a, gain_f, table, router = refs[:9]
    send, keep, row_a, row_f, row_t, rows_r, sems = refs[9:]
    own_rows = row_a.shape[1]
    small = begin(
        [
            pltpu.make_async_copy(source, target, sems.at[4 + i])
            for i, (source, target) in enumerate(
                ((gain_a, row_a), (gain_f, row_f), (table, row_t), (router, rows_r))
            )
        ]
    )
    halves = (keep, send)
    for core in range(2):

        @pl.when(place[0] == core)
        def _(core=core):
            begin(
                [
                    pltpu.make_async_copy(
                        source,
                        halves[(core + i // 2) % 2].at[:, pl.ds(i % 2 * width, width)],
                        sems.at[i],
                    )
                    for i, source in enumerate((query, key, value, out_proj))
                ]
            )

    finish(small)
    columns = [as_column(row_a[...].astype(F32)), as_column(row_f[...].astype(F32))]
    line = row_t[...].astype(F32)
    down = lax.broadcasted_iota(jnp.int32, (own_rows, table_rows), 0)
    across = lax.broadcasted_iota(jnp.int32, (own_rows, table_rows), 1)
    columns.append(jnp.sum(jnp.where(down == across, line, 0.0), axis=1, keepdims=True))
    lines = rows_r[...].astype(F32)
    columns += [as_column(lines[e : e + 1]) for e in range(experts)]
    lane = lax.broadcasted_iota(jnp.int32, (own_rows, EXT), 1)
    block = jnp.zeros((own_rows, EXT), F32)
    for i, column in enumerate(columns):
        block = jnp.where(lane == i, column, block)
    keep[:, 2 * width :] = block.astype(BF)
    send[:, 2 * width :] = block.astype(BF)
    finish(
        [
            pltpu.make_async_copy(source, keep.at[:, pl.ds(0, width)], sems.at[i])
            for i, source in enumerate((query, key, value, out_proj))
        ]
    )


def expert_weights(other, *refs):
    place, keeps, refs = refs[0], refs[1:3], refs[3:]
    if other:
        in_ref, out_ref, held, sem = refs
    else:
        came_in, came_out, in_ref, out_ref, held, sem = refs
    for layer in range(2):

        @pl.when((place[0] == layer) != other)
        def _(layer=layer):
            pltpu.make_async_copy(keeps[layer], held, sem).start()

    pltpu.make_async_copy(keeps[0], held, sem).wait()
    grad_in = t_dot(held[0], held[1])
    grad_out = t_dot(held[2], held[3])
    if not other:
        grad_in = grad_in + came_in[...].astype(F32)
        grad_out = grad_out + came_out[...].astype(F32)
    in_ref[...] = grad_in.astype(in_ref.dtype)
    out_ref[...] = grad_out.astype(out_ref.dtype)


def body(
    feed, segments, routes, rel_bucket, gain_attn, gain_ffn, w_query, w_key, w_value, w_out_attn,
    rel_table, router, expert_in, expert_out,
):
    seq = feed.shape[2]
    width = feed.shape[3]
    experts = lax.axis_size("expert")
    shards = lax.axis_size("shard")
    cap = max(2, 2 * seq // experts)
    own_rows = w_query.shape[1]
    table_rows = rel_table.shape[1]
    quick = direct("expert") and direct("shard")
    blocks_count = experts if quick else 1
    wide = 2 * width + EXT
    side_rows = -(-(LEAD + experts) // 16) * 16
    sec = lax.axis_index("section")
    first = sec == 0
    place = jnp.concatenate(
        [
            jnp.stack([sec, lax.axis_index("expert")]).astype(jnp.int32),
            peer_ids("expert"),
            peer_ids("shard"),
        ]
    )
    row = out((seq, width))
    sems = pltpu.SemaphoreType.DMA

    small = [gain_attn, gain_ffn, rel_table, router[0].T]
    send, kept = call(
        functools.partial(pack_weights, width, experts, table_rows),
        [out((own_rows, wide))] * 2,
        [place, w_query[0], w_key[0], w_value[0], w_out_attn[0], *small],
        [SM] + [HB] * 8,
        [pltpu.VMEM(one.shape, BF) for one in small] + [sems((8,))],
        limit=60,
    )
    came = swap(send)
    part_zero = jnp.where(first, kept, came)

    own_experts = [expert_in[0, 0], expert_out[0, 0]]
    came_experts = [swap(expert_in[0, 0]), swap(expert_out[0, 0])]

    feed_own = feed[0]
    routes_own = routes[0, :, 0]
    layer_x, layer_dy, info = call(
        functools.partial(pick_inputs, seq),
        [row, row, out((8, 2 * seq), jnp.int32)],
        [
            place, feed_own, swap(feed_own), segments[:, 0], routes_own, swap(routes_own),
            rel_bucket[None, :],
        ],
        [SM, HB, AN] + [VM] * 4,
        [sems((2,))],
        after=came_experts,
    )

    infos = spread(info, "shard")


    def both_halves(mine):
        return mine + [swap(piece) for piece in mine]

    def plane_of(part, after=()):
        return call(
            functools.partial(join_rows, shards, 2 + experts),
            [out((shards * own_rows, wide))],
            [place, *spread(part, "shard")],
            [SM] + [VM] * shards,
            after=after,
        )[0]

    half = shards * own_rows // 2
    relay = experts == 4 and half % 16 == 0

    def planes_of(plane):
        if not relay:
            return spread(plane, "expert")
        beside = [hop(plane, "expert", 1), hop(plane, "expert", 2)]
        across = [hop(beside[1][:half], "expert", 1), hop(beside[0][half:], "expert", 2)]
        return [plane, *beside, *across]

    peers = [(i, 0) for i in range(experts)]
    if relay:
        peers = peers + [(experts - 1, half)]
    if quick:
        planes = planes_of(plane_of(part_zero, after=[info]))
        weights_zero = both_halves(planes)
        joined_after = planes[1:3]
        layouts = [peers, ()]
        (part_one,) = call(
            pick_later,
            [out((own_rows, wide))],
            [place, kept, came],
            [SM, VM, VM],
        )
        planes_one = planes_of(plane_of(part_one, after=joined_after))
    else:
        part_one = jnp.where(first, came, kept)
        weights_zero, weights_one = [
            both_halves([lax.all_gather(part, ("expert", "shard"), axis=0, tiled=True)])
            for part in (part_zero, part_one)
        ]
        joined_after = ()
        layouts = [(), ()]


    if quick:
        (slots,) = call(
            functools.partial(routing_slots, shards, seq, experts, cap),
            [out((2 * shards, seq), jnp.int32)],
            [place, *infos],
            [SM] + [VM] * shards,
            after=joined_after,
        )
    else:
        all_routes = jnp.stack([one[1:3, :seq] for one in infos], axis=1)
        hot = (all_routes[..., None] == peer_ids("expert")).astype(BF)
        positions = jnp.arange(seq, dtype=jnp.int32)
        before = (positions[:, None] > positions[None, :]).astype(BF)
        rank = jnp.einsum("ij,lzje->lzie", before, hot, preferred_element_type=F32)
        slot_in = jnp.arange(cap, dtype=jnp.int32).astype(F32)
        back_hot = (hot[..., None] * (rank[..., None] == slot_in).astype(BF)).reshape(
            2, shards, seq, experts * cap
        )
        to_hot = jnp.swapaxes(back_hot, 2, 3)

    block = out((shards * cap * experts // blocks_count, width))
    acts_kind = out((seq, 7 * width))
    probs_kind = out((HEADS // 2, 2 * seq, seq), F32)
    floats_kind = out((seq, width + 2 * EXT), F32)

    def buffer(kind):
        return pltpu.VMEM(kind.shape, kind.dtype)

    expert_scratch = [pltpu.VMEM((2, expert_in.shape[2], expert_in.shape[3]), BF), sems((2,))]
    expert_specs = [SM] + [AN] * 4

    def to_experts(layer, tokens, after=()):
        every = spread(tokens, "shard")
        if not quick:
            slot_rows = jnp.einsum(
                "zcs,zsd->czd", to_hot[layer], jnp.stack(every), preferred_element_type=F32
            )
            slot_rows = slot_rows.astype(BF).reshape(experts, cap * shards, width)
            moved = exchange([slot_rows[i] for i in range(experts)], "expert")
            return [jnp.concatenate(moved, axis=0)]
        blocks = call(
            functools.partial(dispatch_rows, layer, experts, shards, cap),
            [block] * experts,
            [slots, *every],
            [VM] * (1 + shards),
            after=after,
        )
        return exchange(blocks, "expert")

    def to_tokens(layer, blocks, later=(), after=()):
        if not quick:
            rows = blocks[0].reshape(experts, cap * shards, width)
            back = jnp.stack(exchange([rows[i] for i in range(experts)], "expert"))
            back = back.reshape(experts * cap, shards, width)
            tokens = jnp.einsum(
                "zsc,czd->zsd", back_hot[layer], back, preferred_element_type=F32
            ).astype(BF)
            return exchange([tokens[i] for i in range(shards)], "shard"), list(later)
        back = exchange(blocks, "expert")
        results = call(
            functools.partial(combine_rows, layer, experts, shards, cap),
            [row] * shards + [out(one.shape, one.dtype) for one in later],
            [slots, *back, *later],
            [VM] * (1 + experts + len(later)),
            after=after,
        )
        return exchange(results[:shards], "shard"), results[shards:]

    held_kind = out((2, width, wide))

    def attention(layer, pieces, ins, in_specs, after=()):
        count = len(pieces)
        first_outs = [row, row, row] if layer else [row]
        return call(
            functools.partial(
                attn_forward, layer, seq, width, experts, layouts[layer], count, shards, own_rows,
                table_rows,
            ),
            first_outs + [acts_kind, probs_kind, floats_kind, out((width, EXT)), held_kind],
            [place, info, *pieces, *ins],
            [SM, VM] + [VM] * count + in_specs,
            [
                buffer(held_kind), sems(()), buffer(acts_kind),
                buffer(probs_kind), buffer(floats_kind), pltpu.VMEM((width, EXT), BF), buffer(row),
                sems((5,)),
            ],
            out_specs=([VM, VM, HB] if layer else [VM]) + [HB] * 5,
            after=after,
        )

    def attention_back(layer, dy, state, tok, parts, after=()):
        acts, probs, floats, _, held = state
        return call(
            functools.partial(
                attn_backward, layer, seq, width, experts, shards, own_rows, table_rows,
            ),
            [
                row,
                out((seq + side_rows, 4 * width)),
                out((seq, 4 * width)),
                out((side_rows, width), F32),
            ],
            [place, info, held, dy, acts, probs, floats, *tok, *parts],
            [SM, VM, HB, VM] + [HB] * (3 + len(tok)) + [VM] * shards,
            [
                buffer(held_kind), sems(()), buffer(acts_kind),
                buffer(probs_kind), buffer(floats_kind), buffer(row),
                pltpu.VMEM((seq, 3 * width), BF), pltpu.VMEM((16, 2 * seq), F32), sems((4,)),
            ],
            after=after,
        )

    keep_kind = out((4, shards * cap * experts, width))

    def back_expert(layer, rows, dys, ext_side, with_out):
        results = call(
            functools.partial(expert_backward, layer, blocks_count, experts, with_out),
            [block] * (blocks_count * (2 if with_out else 1)) + [keep_kind],
            [place, *own_experts, *came_experts, ext_side, *rows, *dys],
            expert_specs + [HB]
            + ([VM] * blocks_count + [AN] * blocks_count if with_out else [HB] + [VM] * blocks_count),
            expert_scratch + [
                buffer(keep_kind), pltpu.VMEM((width, EXT), BF),
                pltpu.VMEM(keep_kind.shape[1:], BF), sems((1 + 2 * blocks_count,)),
            ],
            out_specs=[VM] * (blocks_count * (2 if with_out else 1)) + [HB],
        )
        return results[:blocks_count], results[blocks_count:-1], results[-1]

    row_parts = experts if quick else 1
    relay = quick and relay

    def cut_of(columns):
        return -(-columns // (2 * EXT)) * EXT

    def weight_blocks(stay, came, parts, sides=(), after=(), later=()):
        columns = len(parts) * (width // 2) + (EXT if sides else 0)
        return call(
            functools.partial(attn_weights, width, row_parts, parts, len(later), relay),
            (
                [out((width // 2, cut_of(columns)))] * 2
                + [out((width // 2, columns - cut_of(columns)))] * 2
                if relay
                else [out((width // row_parts, columns))] * row_parts
            )
            + [out(one.shape, one.dtype) for one in later],
            [place, stay, came, *later, *sides],
            [SM] + [VM] * (2 + len(sides) + len(later)),
            [pltpu.VMEM((width, columns), BF)],
            after=after,
        )

    def sum_planes(blocks, after=()):
        if not quick:
            return blocks
        if relay:
            send_x, kept_x, send_y, kept_y = blocks
            rows, cut, rest = width // 4, kept_x.shape[1], kept_y.shape[1]
            own_x, on_x, own_y, on_y = call(
                halve_sums,
                [out((rows, cut), F32), out((rows, cut)), out((rows, rest), F32), out((rows, rest))],
                [hop(send_x, "expert", 1), kept_x, hop(send_y, "expert", 2), kept_y],
                [VM] * 4,
            )
            return call(
                functools.partial(join_sums, 2 + experts),
                [out((own_rows, cut + rest))] * shards,
                [place, own_x, hop(on_x, "expert", 2), own_y, hop(on_y, "expert", 1)],
                [SM] + [VM] * 4,
                [pltpu.VMEM((rows, cut + rest), F32)],
                after=after,
            )
        columns = blocks[0].shape[1]
        return call(
            functools.partial(sum_blocks, experts, 2 + experts),
            [out((own_rows, columns))] * shards,
            [place, *exchange(blocks, "expert")],
            [SM] + [VM] * experts,
            [pltpu.VMEM((shards * own_rows, columns), F32)],
            after=after,
        )

    def sum_rows(blocks):
        if not quick:
            return scatter_rows(blocks[0])
        columns = blocks[0].shape[1]
        (total,) = call(
            functools.partial(sum_blocks, shards, 0),
            [out((own_rows, columns), F32)],
            [place, *exchange(blocks, "shard")],
            [SM] + [VM] * shards,
            [pltpu.VMEM((own_rows, columns), F32)],
        )
        return total

    n2_zero, *state_zero = attention(
        0, weights_zero, [layer_x], [VM], after=[slots] if quick else ()
    )
    rows_zero = to_experts(0, n2_zero)
    *results, rows_zero = call(
        functools.partial(expert_forward, 0, blocks_count),
        [block] * blocks_count + [out(keep_kind.shape[1:])],
        [place, *own_experts, *came_experts, *rows_zero],
        expert_specs + [VM] * blocks_count,
        expert_scratch + [pltpu.VMEM(keep_kind.shape[1:], BF), sems(())],
        out_specs=[VM] * blocks_count + [HB],
        after=planes_one[1:] if quick else (),
    )
    toks, _ = to_tokens(0, results)
    if quick:
        (gathered,) = call(
            functools.partial(join_planes, peers),
            [out((width, wide))],
            [place, *planes_one],
            [SM] + [VM] * len(planes_one),
            after=results[:1],
        )
        weights_one = both_halves([gathered])
    out_zero, n2_one, tok_zero, *state_one = attention(
        1, weights_one, [state_zero[2], *toks], [HB] + [VM] * shards
    )
    dys_one = to_experts(1, layer_dy)
    rows_one = to_experts(1, n2_one)
    grads, results, keep_one = back_expert(1, rows_one, dys_one, state_one[3], True)
    parts_one, results = to_tokens(1, grads, results)
    toks_one, _ = to_tokens(1, results)
    dx_one, ship_one, stay_one, side_one = attention_back(
        1, layer_dy, state_one, [], parts_one, after=toks_one[:1]
    )
    came_one = swap(ship_one)
    dys_zero = to_experts(0, dx_one)
    out_one, side_one = call(
        functools.partial(last_output, seq, width, experts, shards),
        [row, out((side_rows, width), F32)],
        [info, layer_dy, state_one[0], state_one[2], side_one, *toks_one],
        [VM, VM, HB, HB, VM] + [VM] * shards,
        [buffer(row), buffer(floats_kind), sems((2,))],
    )
    side_one_came = swap(side_one)
    grads, _, keep_zero = back_expert(0, [rows_zero], dys_zero, state_zero[3], False)
    matrix = (expert_in.shape[2], expert_in.shape[3])
    keep_scratch = [pltpu.VMEM(keep_one.shape, BF), sems(())]
    sent = call(
        functools.partial(expert_weights, True),
        [out(matrix)] * 2,
        [place, keep_zero, keep_one],
        [SM, HB, HB],
        keep_scratch,
    )
    came_grads = [swap(grad) for grad in sent]
    parts_zero, _ = to_tokens(0, grads, after=[side_one_came])
    blocks_one = weight_blocks(stay_one, came_one, (0, 1, 2, 3), after=parts_zero[:1])
    dx_zero, ship_zero, stay_zero, side_zero = attention_back(
        0, dx_one, state_zero, [tok_zero], parts_zero, after=[blocks_one[0], sent[0]]
    )
    planes_one_sum = sum_planes(blocks_one)
    came_zero = swap(ship_zero)
    blocks_zero = weight_blocks(
        stay_zero, came_zero, (0, 1, 2, 3), (side_zero, side_one, side_one_came),
        after=planes_one_sum[:1],
    )
    sum_one = sum_rows(planes_one_sum)
    own_grads = call(
        functools.partial(expert_weights, False),
        [out(matrix, F32)] * 2,
        [place, keep_zero, keep_one, *came_grads],
        [SM, HB, HB, VM, VM],
        keep_scratch,
        after=blocks_zero[:1],
    )
    sum_zero = sum_rows(sum_planes(blocks_zero, after=own_grads[:1]))
    (send,) = call(
        functools.partial(last_swap, width),
        [out((own_rows, wide), F32)],
        [place, sum_zero, sum_one],
        [SM] + [VM] * 2,
    )
    matrix_kind = out((own_rows, width), F32)
    weight_grads = call(
        functools.partial(last_grads, width, experts),
        [matrix_kind] * 4
        + [out((1, own_rows), F32)] * 2
        + [out((1, table_rows), F32), out((experts, own_rows), F32)],
        [place, sum_zero, sum_one, swap(send)],
        [SM] + [VM] * 3,
    )

    def by_batch(zero, one):
        came = swap(jnp.where(first, one, zero))
        kept = jnp.where(first, zero, one)
        return jnp.stack([jnp.where(first, kept, came), jnp.where(first, came, kept)])

    grad_query, grad_key, grad_value, grad_out, grad_a, grad_f, grad_table, grad_router = weight_grads
    return (
        by_batch(out_zero, out_one)[None],
        by_batch(dx_zero, dx_one)[None],
        grad_a,
        grad_f,
        grad_query[None],
        grad_key[None],
        grad_value[None],
        grad_out[None],
        grad_table,
        grad_router.T[None],
        own_grads[0][None, None],
        own_grads[1][None, None],
    )


def solution(mesh):
    rows = ("expert", "shard")
    tokens = P("section", None, rows, None)
    matrix = P("section", rows, None)
    vector = P("section", rows)
    expert_specs = (P("section", "expert", None, "shard"), P("section", "expert", "shard", None))
    in_specs = (
        tokens, P(None, rows, None), tokens, P(), vector, vector, matrix, matrix, matrix, matrix,
        vector, matrix, *expert_specs,
    )
    out_specs = (
        tokens, tokens, vector, vector, matrix, matrix, matrix, matrix, vector, matrix,
        *expert_specs,
    )
    return jax.shard_map(body, mesh=mesh, in_specs=in_specs, out_specs=out_specs, check_vma=False)
```

profile of v0, /device:TPU:1, one launch (start us, length us, event | category | flops | bytes accessed | tf_op | source)
XLA Modules:
  0.0 317.8 jit_solution(5233686658247468633)
XLA Ops:
  1.8 2.5 shard_map.230
  6.0 4.5 %collective-permute-start.10 = (bf16[48,1664]{1,0:T(8,128)(2,1)S(1)}, bf16[48,1664]{1,0:T(8,128)(2,1)S(1)}, u32[]{:S(2)}, u32[]{:S(2)}) collective-permute-start(bf16[48,1664]{1,0:T(8,128)(2,1)S(1)} %broadcast_select_fusion.refs_1_), channel_id=1, source_target_pairs={{0,3},{1,2},{2,1},{3,0},{4,7},{5,6},{6,5},{7,4},{8,11},{9,10},{10,... | collective-permute-start | bytes 479240 | tf_op jit(solution)/shard_map/ppermute | solution.py:56
  15.6 2.9 collective-permute-done.8.refs_2_
  18.5 5.1 %collective-permute-done.9.refs_3_ = bf16[48,1664]{1,0:T(8,128)(2,1)S(1)} collective-permute-done((bf16[48,1664]{1,0:T(8,128)(2,1)S(1)}, bf16[48,1664]{1,0:T(8,128)(2,1)S(1)}, u32[]{:S(2)}, u32[]{:S(2)}) %collective-permute-start.9) | collective-permute-done | bytes 159776 | tf_op jit(solution)/shard_map/ppermute | solution.py:56
  30.9 7.8 %collective-permute-done.12.refs_6_.refs_4_ = bf16[192,1664]{1,0:T(8,128)(2,1)S(1)} collective-permute-done((bf16[192,1664]{1,0:T(8,128)(2,1)S(1)}, bf16[192,1664]{1,0:T(8,128)(2,1)S(1)}, u32[]{:S(2)}, u32[]{:S(2)}) %collective-permute-start.12) | collective-permute-done | bytes 639008 | tf_op jit(solution)/shard_map/ppermute | solution.py:56
  47.4 2.1 collective-permute-done.18.refs_3_
  50.7 3.1 collective-permute-done.19.refs_4_
  53.7 6.7 %collective-permute-start.22 = (bf16[192,1664]{1,0:T(8,128)(2,1)S(1)}, bf16[192,1664]{1,0:T(8,128)(2,1)S(1)}, u32[]{:S(2)}, u32[]{:S(2)}) collective-permute-start(bf16[192,1664]{1,0:T(8,128)(2,1)S(1)} %shard_map.232.refs_2_), channel_id=1, source_target_pairs={{0,16},{16,0},{1,17},{17,1},{2,18},{18,2},{3,19},{19,3},{4,20},{20... | collective-permute-start | bytes 1916936 | tf_op jit(solution)/shard_map/ppermute | solution.py:40
  61.0 2.8 collective-permute-start.25
  66.2 4.7 %shard_map.235 = (bf16[64,768]{1,0:T(8,128)(2,1)S(1)}, bf16[64,5376]{1,0:T(8,128)(2,1)S(1)}, f32[6,128,64]{2,1,0:T(8,128)S(1)}, f32[64,1024]{1,0:T(8,128)S(1)}, ...) custom-call(s32[10]{0:T(128)S(1)} %copy-done.4, s32[8,128]{1,0:T(8,128)S(1)} %get-tuple-element.132.refs_5_.refs_1_.refs_0_, ...), custom_call_target="tpu_custom_call" | custom-call | bytes 11767848 | tf_op jit(solution)/shard_map/pallas_call | solution.py:95
  75.5 3.1 collective-permute-done.29.refs_4_
  83.5 3.6 %collective-permute-done.31.refs_7_ = bf16[128,768]{1,0:T(8,128)(2,1)S(1)} collective-permute-done((bf16[128,768]{1,0:T(8,128)(2,1)S(1)}, bf16[128,768]{1,0:T(8,128)(2,1)S(1)}, u32[]{:S(2)}, u32[]{:S(2)}) %collective-permute-start.31) | collective-permute-done | bytes 196640 | tf_op jit(solution)/shard_map/ppermute | solution.py:56
  87.1 3.6 %shard_map.237 = (bf16[128,768]{1,0:T(8,128)(2,1)S(1)}, bf16[128,768]{1,0:T(8,128)(2,1)S(1)}, bf16[128,768]{1,0:T(8,128)(2,1)S(1)}, bf16[128,768]{1,0:T(8,128)(2,1)S(1)}, bf16[512,768]{1,0:T(8,128)(2,1)S(1)}) custom-call(s32[10]{0:T(128)S(1)} %copy-done.4, bf16[768,768]{1,0:T(8,128)(2,1)S(1)} %bitcast.37, bf16[768,768]{1,0:T(8,128)(2,1)S(1)} %bitcast.41, ...), custom_call_target="tpu_custom_call" | custom-call | bytes 7077928 | tf_op jit(solution)/shard_map/pallas_call | solution.py:95
  91.5 5.1 %collective-permute-start.33 = (bf16[768,1664]{1,0:T(8,128)(2,1)S(1)}, bf16[768,1664]{1,0:T(8,128)(2,1)S(1)}, u32[]{:S(2)}, u32[]{:S(2)}) collective-permute-start(bf16[768,1664]{1,0:T(8,128)(2,1)S(1)} %shard_map.238.refs_2_), channel_id=1, source_target_pairs={{0,16},{16,0},{1,17},{17,1},{2,18},{18,2},{3,19},{19,3},{4,20},{20... | collective-permute-start | bytes 7667720 | tf_op jit(solution)/shard_map/ppermute | solution.py:40
  99.3 2.8 collective-permute-start.46
  103.1 3.0 collective-permute-start.47
  108.3 2.4 collective-permute-start.37
  115.8 3.6 %collective-permute-done.38.refs_7_ = bf16[64,768]{1,0:T(8,128)(2,1)S(1)} collective-permute-done((bf16[64,768]{1,0:T(8,128)(2,1)S(1)}, bf16[64,768]{1,0:T(8,128)(2,1)S(1)}, u32[]{:S(2)}, u32[]{:S(2)}) %collective-permute-start.38) | collective-permute-done | bytes 98336 | tf_op jit(solution)/shard_map/ppermute | solution.py:56
  119.4 5.1 %shard_map.240 = (bf16[64,768]{1,0:T(8,128)(2,1)S(1)}, bf16[64,768]{1,0:T(8,128)(2,1)S(1)}, bf16[64,768]{1,0:T(8,128)(2,1)S(1)}, bf16[64,5376]{1,0:T(8,128)(2,1)...) custom-call(s32[10]{0:T(128)S(1)} %copy-done.4, ...), custom_call_target="tpu_custom_call" | custom-call | bytes 12521512 | tf_op jit(solution)/shard_map/pallas_call | solution.py:95
  124.5 3.5 %collective-permute-start.40 = (bf16[64,768]{1,0:T(8,128)(2,1)S(1)}, bf16[64,768]{1,0:T(8,128)(2,1)S(1)}, u32[]{:S(2)}, u32[]{:S(2)}) collective-permute-start(bf16[64,768]{1,0:T(8,128)(2,1)S(1)} %get-tuple-element.157.refs_1_), channel_id=1, source_target_pairs={{0,1},{1,0},{2,3},{3,2},{4,5},{5,4},{6,7},{7,6},{8,9},{9,8},{10,11... | collective-permute-start | bytes 294920 | tf_op jit(solution)/shard_map/ppermute | solution.py:56
  132.7 2.2 collective-permute-done.41.refs_3_
  136.6 2.3 collective-permute-start.44
  140.9 7.6 %collective-permute-done.44.refs_8_ = bf16[128,768]{1,0:T(8,128)(2,1)S(1)} collective-permute-done((bf16[128,768]{1,0:T(8,128)(2,1)S(1)}, bf16[128,768]{1,0:T(8,128)(2,1)S(1)}, u32[]{:S(2)}, u32[]{:S(2)}) %collective-permute-start.44) | collective-permute-done | bytes 196640 | tf_op jit(solution)/shard_map/ppermute | solution.py:56
  148.6 11.2 %shard_map.243 = (bf16[128,768]{1,0:T(8,128)(2,1)S(1)}, bf16[128,768]{1,0:T(8,128)(2,1)S(1)}, bf16[128,768]{1,0:T(8,128)(2,1)S(1)}, bf16[128,768]{1,0:T(8,128)(2...) custom-call(s32[10]{0:T(128)S(1)} %copy-done.4, ...), custom_call_target="tpu_custom_call" | custom-call | bytes 11206696 | tf_op jit(solution)/shard_map/pallas_call | solution.py:95
  159.8 2.4 collective-permute-start.53
  164.3 2.7 collective-permute-done.53.refs_3_
  167.1 4.1 %collective-permute-done.54.refs_4_ = bf16[128,768]{1,0:T(8,128)(2,1)S(1)} collective-permute-done((bf16[128,768]{1,0:T(8,128)(2,1)S(1)}, bf16[128,768]{1,0:T(8,128)(2,1)S(1)}, u32[]{:S(2)}, u32[]{:S(2)}) %collective-permute-start.54) | collective-permute-done | bytes 196640 | tf_op jit(solution)/shard_map/ppermute | solution.py:56
  171.7 2.5 collective-permute-start.60
  179.7 2.7 collective-permute-done.57.refs_10_
  182.4 5.9 %shard_map.246 = (bf16[64,768]{1,0:T(8,128)(2,1)S(1)}, bf16[80,3072]{1,0:T(8,128)(2,1)S(1)}, bf16[64,3072]{1,0:T(8,128)(2,1)S(1)}, f32[16,768]{1,0:T(8,128)S(1)}) custom-call(s32[10]{0:T(128)S(1)} %copy-done.4, s32[8,128]{1,0:T(8,128)S(1)} %get-tuple-element.132.refs_5_.refs_1_.refs_0_, bf16[2,768,1664]{2,1,0:T(8,128)(2,1)S(1)} %get-tuple-element.154.refs_2_, ...), custom_call_target="tpu_custom_call" | custom-call | bytes 7786536 | tf_op jit(solution)/shard_map/pallas_call | solution.py:95
  191.9 5.8 %collective-permute-start.78 = (bf16[80,3072]{1,0:T(8,128)(2,1)S(1)}, bf16[80,3072]{1,0:T(8,128)(2,1)S(1)}, u32[]{:S(2)}, u32[]{:S(2)}) collective-permute-start(bf16[80,3072]{1,0:T(8,128)(2,1)S(1)} %get-tuple-element.209), channel_id=1, source_target_pairs={{0,16},{16,0},{1,17},{17,1},{2,18},{18,2},{3,19},{19,3},{4,20},{20... | collective-permute-start | bytes 1474568 | tf_op jit(solution)/shard_map/ppermute | solution.py:40
  202.6 2.9 collective-permute-done.69.refs_9_
  205.6 7.4 %shard_map.249 = (bf16[128,768]{1,0:T(8,128)(2,1)S(1)}, bf16[128,768]{1,0:T(8,128)(2,1)S(1)}, bf16[128,768]{1,0:T(8,128)(2,1)S(1)}, bf16[128,768]{1,0:T(8,128)(2,1)S(1)}, bf16[4,512,768]{2,1,0:T(8,128)(2,1)S(1)}) custom-call(s32[10]{0:T(128)S(1)} %copy-done.4, bf16[768,768]{1,0:T(8,128)(2,1)S(1)} %bitcast.39, bf16[768,768]{1,0:T(8,128)(2,1)S(1)} %bitcast.43, ...), custom_call_target="tpu_custom_call" | custom-call | bytes 10420264 | tf_op jit(solution)/shard_map/pallas_call | solution.py:95
  215.7 5.2 %collective-permute-done.63.refs_8_ = bf16[64,768]{1,0:T(8,128)(2,1)S(1)} collective-permute-done((bf16[64,768]{1,0:T(8,128)(2,1)S(1)}, bf16[64,768]{1,0:T(8,128)(2,1)S(1)}, u32[]{:S(2)}, u32[]{:S(2)}) %collective-permute-start.63) | collective-permute-done | bytes 98336 | tf_op jit(solution)/shard_map/ppermute | solution.py:56
  221.5 6.9 %collective-permute-start.74 = (f32[16,768]{1,0:T(8,128)S(1)}, f32[16,768]{1,0:T(8,128)S(1)}, u32[]{:S(2)}, u32[]{:S(2)}) collective-permute-start(f32[16,768]{1,0:T(8,128)S(1)} %get-tuple-element.203.refs_4_), channel_id=1, source_target_pairs={{0,16},{16,0},{1,17},{17,1},{2,18},{18,2},{3,19},{19,3},{4,20},{20... | collective-permute-start | bytes 147464 | tf_op jit(solution)/shard_map/ppermute | solution.py:40
  229.6 2.1 shard_map.251
  233.4 2.6 collective-permute-start.76
  236.9 2.2 shard_map.252
  239.1 3.0 collective-permute-done.77.refs_11_
  242.1 5.9 %shard_map.253 = (bf16[64,768]{1,0:T(8,128)(2,1)S(1)}, bf16[80,3072]{1,0:T(8,128)(2,1)S(1)}, bf16[64,3072]{1,0:T(8,128)(2,1)S(1)}, f32[16,768]{1,0:T(8,128)S(1)}) custom-call(s32[10]{0:T(128)S(1)} %copy-done.4, s32[8,128]{1,0:T(8,128)S(1)} %get-tuple-element.132.refs_5_.refs_1_.refs_0_, bf16[2,768,1664]{2,1,0:T(8,128)(2,1)S(1)} %get-tuple-element.188.refs_2_, ...), custom_call_target="tpu_custom_call" | custom-call | bytes 7884840 | tf_op jit(solution)/shard_map/pallas_call | solution.py:95
  247.9 3.0 collective-permute-start.80
  252.7 7.1 %collective-permute-done.83.refs_2_ = bf16[192,768]{1,0:T(8,128)(2,1)S(1)} collective-permute-done((bf16[192,768]{1,0:T(8,128)(2,1)S(1)}, bf16[192,768]{1,0:T(8,128)(2,1)S(1)}, u32[]{:S(2)}, u32[]{:S(2)}) %collective-permute-start.83) | collective-permute-done | bytes 294944 | tf_op jit(solution)/shard_map/ppermute | solution.py:56
  261.2 2.7 shard_map.256
  266.6 13.8 %collective-permute-done.86.refs_2_ = bf16[384,768]{1,0:T(8,128)(2,1)S(1)} collective-permute-done((bf16[384,768]{1,0:T(8,128)(2,1)S(1)}, bf16[384,768]{1,0:T(8,128)(2,1)S(1)}, u32[]{:S(2)}, u32[]{:S(2)}) %collective-permute-start.86) | collective-permute-done | bytes 589856 | tf_op jit(solution)/shard_map/ppermute | solution.py:56
  287.7 4.0 %shard_map.258 = (f32[768,768]{1,0:T(8,128)}, f32[768,768]{1,0:T(8,128)}) custom-call(s32[10]{0:T(128)S(1)} %copy-done.5, bf16[4,512,768]{2,1,0:T(8,128)(2,1)S(1)} %get-tuple-element.211.refs_1_, bf16[4,512,768]{2,1,0:T(8,128)(2,1)S(1)} %get-tuple-element.212.refs_2_, bf16[768,768]{1,0:T(8,128)(2,1)S(1)} %collective-permute-done.89.refs_3_, ...), custom_call_target="tpu_custom_call" | custom-call | bytes 13369384 | tf_op jit(solution)/shard_map/pallas_call | solution.py:95
  297.8 2.3 collective-permute-start.79
  303.0 8.0 %collective-permute-done.92.refs_3_ = bf16[48,1664]{1,0:T(8,128)(2,1)S(1)} collective-permute-done((bf16[48,1664]{1,0:T(8,128)(2,1)S(1)}, bf16[48,1664]{1,0:T(8,128)(2,1)S(1)}, u32[]{:S(2)}, u32[]{:S(2)}) %collective-permute-start.92) | collective-permute-done | bytes 159776 | tf_op jit(solution)/shard_map/ppermute | solution.py:56
  312.2 2.6 collective-permute-start.97
  (216 shorter events, 107.1 us)
Async XLA Ops:
  0.6 10.5 %collective-permute-start.2 = (bf16[768,768]{1,0:T(8,128)(2,1)}, bf16[768,768]{1,0:T(8,128)(2,1)S(1)}, u32[]{:S(2)}, u32[]{:S(2)}) collective-permute-start(bf16[768,768]{1,0:T(8,128)(2,1)} %bitcast.36), channel_id=1, source_target_pairs={{0,16},{16,0},{1,17},{17,1},{2,18},{18,2},{3,19},{19,3},{4,20},{20... | collective-permute-start | bytes 3538952 | tf_op jit(solution)/shard_map/ppermute | solution.py:40
  0.8 10.4 %collective-permute-start.3 = (bf16[768,768]{1,0:T(8,128)(2,1)}, bf16[768,768]{1,0:T(8,128)(2,1)S(1)}, u32[]{:S(2)}, u32[]{:S(2)}) collective-permute-start(bf16[768,768]{1,0:T(8,128)(2,1)} %bitcast.40), channel_id=1, source_target_pairs={{0,16},{16,0},{1,17},{17,1},{2,18},{18,2},{3,19},{19,3},{4,20},{20... | collective-permute-start | bytes 3538952 | tf_op jit(solution)/shard_map/ppermute | solution.py:40
  6.0 9.6 %collective-permute-start.10 = (bf16[48,1664]{1,0:T(8,128)(2,1)S(1)}, bf16[48,1664]{1,0:T(8,128)(2,1)S(1)}, u32[]{:S(2)}, u32[]{:S(2)}) collective-permute-start(bf16[48,1664]{1,0:T(8,128)(2,1)S(1)} %broadcast_select_fusion.refs_1_), channel_id=1, source_target_pairs={{0,3},{1,2},{2,1},{3,0},{4,7},{5,6},{6,5},{7,4},{8,11},{9,10},{10,... | collective-permute-start | bytes 479240 | tf_op jit(solution)/shard_map/ppermute | solution.py:56
  10.6 13.1 %collective-permute-start.9 = (bf16[48,1664]{1,0:T(8,128)(2,1)S(1)}, bf16[48,1664]{1,0:T(8,128)(2,1)S(1)}, u32[]{:S(2)}, u32[]{:S(2)}) collective-permute-start(bf16[48,1664]{1,0:T(8,128)(2,1)S(1)} %broadcast_select_fusion.refs_1_), channel_id=1, source_target_pairs={{0,2},{1,3},{2,0},{3,1},{4,6},{5,7},{6,4},{7,5},{8,10},{9,11},{10,... | collective-permute-start | bytes 479240 | tf_op jit(solution)/shard_map/ppermute | solution.py:56
  24.2 14.5 %collective-permute-start.12 = (bf16[192,1664]{1,0:T(8,128)(2,1)S(1)}, bf16[192,1664]{1,0:T(8,128)(2,1)S(1)}, u32[]{:S(2)}, u32[]{:S(2)}) collective-permute-start(bf16[192,1664]{1,0:T(8,128)(2,1)S(1)} %shard_map.232.refs_2_), channel_id=1, source_target_pairs={{0,8},{4,12},{8,0},{12,4},{1,9},{5,13},{9,1},{13,5},{2,10},{6,14},... | collective-permute-start | bytes 1916936 | tf_op jit(solution)/shard_map/ppermute | solution.py:56
  25.5 14.5 %collective-permute-start.11 = (bf16[192,1664]{1,0:T(8,128)(2,1)S(1)}, bf16[192,1664]{1,0:T(8,128)(2,1)S(1)}, u32[]{:S(2)}, u32[]{:S(2)}) collective-permute-start(bf16[192,1664]{1,0:T(8,128)(2,1)S(1)} %shard_map.232.refs_2_), channel_id=1, source_target_pairs={{0,4},{4,0},{8,12},{12,8},{1,5},{5,1},{9,13},{13,9},{2,6},{6,2},{1... | collective-permute-start | bytes 1916936 | tf_op jit(solution)/shard_map/ppermute | solution.py:56
  27.3 14.1 %collective-permute-start.5 = (bf16[48,1664]{1,0:T(8,128)(2,1)S(1)}, bf16[48,1664]{1,0:T(8,128)(2,1)S(1)}, u32[]{:S(2)}, u32[]{:S(2)}) collective-permute-start(bf16[48,1664]{1,0:T(8,128)(2,1)S(1)} %shard_map.231.refs_1_), channel_id=1, source_target_pairs={{0,1},{1,0},{2,3},{3,2},{4,5},{5,4},{6,7},{7,6},{8,9},{9,8},{10,11... | collective-permute-start | bytes 479240 | tf_op jit(solution)/shard_map/ppermute | solution.py:56
  27.4 14.0 %collective-permute-start.6 = (bf16[48,1664]{1,0:T(8,128)(2,1)S(1)}, bf16[48,1664]{1,0:T(8,128)(2,1)S(1)}, u32[]{:S(2)}, u32[]{:S(2)}) collective-permute-start(bf16[48,1664]{1,0:T(8,128)(2,1)S(1)} %shard_map.231.refs_1_), channel_id=1, source_target_pairs={{0,2},{1,3},{2,0},{3,1},{4,6},{5,7},{6,4},{7,5},{8,10},{9,11},{10,... | collective-permute-start | bytes 479240 | tf_op jit(solution)/shard_map/ppermute | solution.py:56
  29.5 11.9 %collective-permute-start.7 = (bf16[48,1664]{1,0:T(8,128)(2,1)S(1)}, bf16[48,1664]{1,0:T(8,128)(2,1)S(1)}, u32[]{:S(2)}, u32[]{:S(2)}) collective-permute-start(bf16[48,1664]{1,0:T(8,128)(2,1)S(1)} %shard_map.231.refs_1_), channel_id=1, source_target_pairs={{0,3},{1,2},{2,1},{3,0},{4,7},{5,6},{6,5},{7,4},{8,11},{9,10},{10,... | collective-permute-start | bytes 479240 | tf_op jit(solution)/shard_map/ppermute | solution.py:56
  38.8 21.7 %collective-permute-start.20 = (bf16[96,1664]{1,0:T(8,128)(2,1)S(1)}, bf16[96,1664]{1,0:T(8,128)(2,1)S(1)}, u32[]{:S(2)}, u32[]{:S(2)}) collective-permute-start(bf16[96,1664]{1,0:T(8,128)(2,1)S(1)} %slice.18), channel_id=1, source_target_pairs={{0,4},{4,0},{8,12},{12,8},{1,5},{5,1},{9,13},{13,9},{2,6},{6,2},{1... | collective-permute-start | bytes 958472 | tf_op jit(solution)/shard_map/ppermute | solution.py:56
  40.1 20.4 %collective-permute-start.21 = (bf16[96,1664]{1,0:T(8,128)(2,1)S(1)}, bf16[96,1664]{1,0:T(8,128)(2,1)S(1)}, u32[]{:S(2)}, u32[]{:S(2)}) collective-permute-start(bf16[96,1664]{1,0:T(8,128)(2,1)S(1)} %slice.19), channel_id=1, source_target_pairs={{0,8},{4,12},{8,0},{12,4},{1,9},{5,13},{9,1},{13,5},{2,10},{6,14},... | collective-permute-start | bytes 958472 | tf_op jit(solution)/shard_map/ppermute | solution.py:56
  42.0 19.0 %collective-permute-start.14 = (bf16[192,1664]{1,0:T(8,128)(2,1)S(1)}, bf16[192,1664]{1,0:T(8,128)(2,1)S(1)}, u32[]{:S(2)}, u32[]{:S(2)}) collective-permute-start(bf16[192,1664]{1,0:T(8,128)(2,1)S(1)} %shard_map.233.refs_1_), channel_id=1, source_target_pairs={{0,8},{4,12},{8,0},{12,4},{1,9},{5,13},{9,1},{13,5},{2,10},{6,14},... | collective-permute-start | bytes 1916936 | tf_op jit(solution)/shard_map/ppermute | solution.py:56
  42.3 21.5 %collective-permute-start.13 = (bf16[192,1664]{1,0:T(8,128)(2,1)S(1)}, bf16[192,1664]{1,0:T(8,128)(2,1)S(1)}, u32[]{:S(2)}, u32[]{:S(2)}) collective-permute-start(bf16[192,1664]{1,0:T(8,128)(2,1)S(1)} %shard_map.233.refs_1_), channel_id=1, source_target_pairs={{0,4},{4,0},{8,12},{12,8},{1,5},{5,1},{9,13},{13,9},{2,6},{6,2},{1... | collective-permute-start | bytes 1916936 | tf_op jit(solution)/shard_map/ppermute | solution.py:56
  53.7 10.1 %collective-permute-start.22 = (bf16[192,1664]{1,0:T(8,128)(2,1)S(1)}, bf16[192,1664]{1,0:T(8,128)(2,1)S(1)}, u32[]{:S(2)}, u32[]{:S(2)}) collective-permute-start(bf16[192,1664]{1,0:T(8,128)(2,1)S(1)} %shard_map.232.refs_2_), channel_id=1, source_target_pairs={{0,16},{16,0},{1,17},{17,1},{2,18},{18,2},{3,19},{19,3},{4,20},{20... | collective-permute-start | bytes 1916936 | tf_op jit(solution)/shard_map/ppermute | solution.py:40
  63.9 23.2 %collective-permute-start.15 = (bf16[96,1664]{1,0:T(8,128)(2,1)S(1)}, bf16[96,1664]{1,0:T(8,128)(2,1)S(1)}, u32[]{:S(2)}, u32[]{:S(2)}) collective-permute-start(bf16[96,1664]{1,0:T(8,128)(2,1)S(1)} %slice.16), channel_id=1, source_target_pairs={{0,4},{4,0},{8,12},{12,8},{1,5},{5,1},{9,13},{13,9},{2,6},{6,2},{1... | collective-permute-start | bytes 958472 | tf_op jit(solution)/shard_map/ppermute | solution.py:56
  64.8 22.3 %collective-permute-start.16 = (bf16[96,1664]{1,0:T(8,128)(2,1)S(1)}, bf16[96,1664]{1,0:T(8,128)(2,1)S(1)}, u32[]{:S(2)}, u32[]{:S(2)}) collective-permute-start(bf16[96,1664]{1,0:T(8,128)(2,1)S(1)} %slice.17), channel_id=1, source_target_pairs={{0,8},{4,12},{8,0},{12,4},{1,9},{5,13},{9,1},{13,5},{2,10},{6,14},... | collective-permute-start | bytes 958472 | tf_op jit(solution)/shard_map/ppermute | solution.py:56
  91.5 27.9 %collective-permute-start.33 = (bf16[768,1664]{1,0:T(8,128)(2,1)S(1)}, bf16[768,1664]{1,0:T(8,128)(2,1)S(1)}, u32[]{:S(2)}, u32[]{:S(2)}) collective-permute-start(bf16[768,1664]{1,0:T(8,128)(2,1)S(1)} %shard_map.238.refs_2_), channel_id=1, source_target_pairs={{0,16},{16,0},{1,17},{17,1},{2,18},{18,2},{3,19},{19,3},{4,20},{20... | collective-permute-start | bytes 7667720 | tf_op jit(solution)/shard_map/ppermute | solution.py:40
  96.9 9.2 %collective-permute-start.35 = (bf16[128,768]{1,0:T(8,128)(2,1)S(1)}, bf16[128,768]{1,0:T(8,128)(2,1)S(1)}, u32[]{:S(2)}, u32[]{:S(2)}) collective-permute-start(bf16[128,768]{1,0:T(8,128)(2,1)S(1)} %get-tuple-element.144), channel_id=1, source_target_pairs={{0,8},{4,12},{8,0},{12,4},{1,9},{5,13},{9,1},{13,5},{2,10},{6,14},... | collective-permute-start | bytes 589832 | tf_op jit(solution)/shard_map/ppermute | solution.py:56
  97.7 10.3 %collective-permute-start.36 = (bf16[128,768]{1,0:T(8,128)(2,1)S(1)}, bf16[128,768]{1,0:T(8,128)(2,1)S(1)}, u32[]{:S(2)}, u32[]{:S(2)}) collective-permute-start(bf16[128,768]{1,0:T(8,128)(2,1)S(1)} %get-tuple-element.145), channel_id=1, source_target_pairs={{0,12},{4,8},{8,4},{12,0},{1,13},{5,9},{9,5},{13,1},{2,14},{6,10},... | collective-permute-start | bytes 589832 | tf_op jit(solution)/shard_map/ppermute | solution.py:56
  99.3 11.5 %collective-permute-start.46 = (bf16[64,768]{1,0:T(8,128)(2,1)S(1)}, bf16[64,768]{1,0:T(8,128)(2,1)S(1)}, u32[]{:S(2)}, u32[]{:S(2)}) collective-permute-start(bf16[64,768]{1,0:T(8,128)(2,1)S(1)} %get-tuple-element.151.refs_1_.refs_3_), channel_id=1, source_target_pairs={{0,1},{1,0},{2,3},{3,2},{4,5},{5,4},{6,7},{7,6},{8,9},{9,8},{10,11... | collective-permute-start | bytes 294920 | tf_op jit(solution)/shard_map/ppermute | solution.py:56
  113.3 25.6 %collective-permute-start.49 = (bf16[128,768]{1,0:T(8,128)(2,1)S(1)}, bf16[128,768]{1,0:T(8,128)(2,1)S(1)}, u32[]{:S(2)}, u32[]{:S(2)}) collective-permute-start(bf16[128,768]{1,0:T(8,128)(2,1)S(1)} %get-tuple-element.163), channel_id=1, source_target_pairs={{0,4},{4,0},{8,12},{12,8},{1,5},{5,1},{9,13},{13,9},{2,6},{6,2},{1... | collective-permute-start | bytes 589832 | tf_op jit(solution)/shard_map/ppermute | solution.py:56
  130.2 9.8 %collective-permute-start.50 = (bf16[128,768]{1,0:T(8,128)(2,1)S(1)}, bf16[128,768]{1,0:T(8,128)(2,1)S(1)}, u32[]{:S(2)}, u32[]{:S(2)}) collective-permute-start(bf16[128,768]{1,0:T(8,128)(2,1)S(1)} %get-tuple-element.164), channel_id=1, source_target_pairs={{0,8},{4,12},{8,0},{12,4},{1,9},{5,13},{9,1},{13,5},{2,10},{6,14},... | collective-permute-start | bytes 589832 | tf_op jit(solution)/shard_map/ppermute | solution.py:56
  136.6 12.0 %collective-permute-start.44 = (bf16[128,768]{1,0:T(8,128)(2,1)S(1)}, bf16[128,768]{1,0:T(8,128)(2,1)S(1)}, u32[]{:S(2)}, u32[]{:S(2)}) collective-permute-start(bf16[128,768]{1,0:T(8,128)(2,1)S(1)} %get-tuple-element.160), channel_id=1, source_target_pairs={{0,8},{4,12},{8,0},{12,4},{1,9},{5,13},{9,1},{13,5},{2,10},{6,14},... | collective-permute-start | bytes 589832 | tf_op jit(solution)/shard_map/ppermute | solution.py:56
  138.9 9.7 %collective-permute-start.45 = (bf16[128,768]{1,0:T(8,128)(2,1)S(1)}, bf16[128,768]{1,0:T(8,128)(2,1)S(1)}, u32[]{:S(2)}, u32[]{:S(2)}) collective-permute-start(bf16[128,768]{1,0:T(8,128)(2,1)S(1)} %get-tuple-element.161), channel_id=1, source_target_pairs={{0,12},{4,8},{8,4},{12,0},{1,13},{5,9},{9,5},{13,1},{2,14},{6,10},... | collective-permute-start | bytes 589832 | tf_op jit(solution)/shard_map/ppermute | solution.py:56
  162.3 8.9 %collective-permute-start.54 = (bf16[128,768]{1,0:T(8,128)(2,1)S(1)}, bf16[128,768]{1,0:T(8,128)(2,1)S(1)}, u32[]{:S(2)}, u32[]{:S(2)}) collective-permute-start(bf16[128,768]{1,0:T(8,128)(2,1)S(1)} %get-tuple-element.169), channel_id=1, source_target_pairs={{0,12},{4,8},{8,4},{12,0},{1,13},{5,9},{9,5},{13,1},{2,14},{6,10},... | collective-permute-start | bytes 589832 | tf_op jit(solution)/shard_map/ppermute | solution.py:56
  188.3 9.4 %collective-permute-start.65 = (bf16[64,768]{1,0:T(8,128)(2,1)S(1)}, bf16[64,768]{1,0:T(8,128)(2,1)S(1)}, u32[]{:S(2)}, u32[]{:S(2)}) collective-permute-start(bf16[64,768]{1,0:T(8,128)(2,1)S(1)} %get-tuple-element.189.refs_1_.refs_3_), channel_id=1, source_target_pairs={{0,1},{1,0},{2,3},{3,2},{4,5},{5,4},{6,7},{7,6},{8,9},{9,8},{10,11... | collective-permute-start | bytes 294920 | tf_op jit(solution)/shard_map/ppermute | solution.py:56
  188.4 9.3 %collective-permute-start.66 = (bf16[64,768]{1,0:T(8,128)(2,1)S(1)}, bf16[64,768]{1,0:T(8,128)(2,1)S(1)}, u32[]{:S(2)}, u32[]{:S(2)}) collective-permute-start(bf16[64,768]{1,0:T(8,128)(2,1)S(1)} %get-tuple-element.189.refs_1_.refs_3_), channel_id=1, source_target_pairs={{0,2},{1,3},{2,0},{3,1},{4,6},{5,7},{6,4},{7,5},{8,10},{9,11},{10,... | collective-permute-start | bytes 294920 | tf_op jit(solution)/shard_map/ppermute | solution.py:56
  191.9 37.7 %collective-permute-start.78 = (bf16[80,3072]{1,0:T(8,128)(2,1)S(1)}, bf16[80,3072]{1,0:T(8,128)(2,1)S(1)}, u32[]{:S(2)}, u32[]{:S(2)}) collective-permute-start(bf16[80,3072]{1,0:T(8,128)(2,1)S(1)} %get-tuple-element.209), channel_id=1, source_target_pairs={{0,16},{16,0},{1,17},{17,1},{2,18},{18,2},{3,19},{19,3},{4,20},{20... | collective-permute-start | bytes 1474568 | tf_op jit(solution)/shard_map/ppermute | solution.py:40
  200.8 13.2 %collective-permute-start.61 = (bf16[64,768]{1,0:T(8,128)(2,1)S(1)}, bf16[64,768]{1,0:T(8,128)(2,1)S(1)}, u32[]{:S(2)}, u32[]{:S(2)}) collective-permute-start(bf16[64,768]{1,0:T(8,128)(2,1)S(1)} %get-tuple-element.184), channel_id=1, source_target_pairs={{0,1},{1,0},{2,3},{3,2},{4,5},{5,4},{6,7},{7,6},{8,9},{9,8},{10,11... | collective-permute-start | bytes 294920 | tf_op jit(solution)/shard_map/ppermute | solution.py:56
  202.6 13.0 %collective-permute-start.62 = (bf16[64,768]{1,0:T(8,128)(2,1)S(1)}, bf16[64,768]{1,0:T(8,128)(2,1)S(1)}, u32[]{:S(2)}, u32[]{:S(2)}) collective-permute-start(bf16[64,768]{1,0:T(8,128)(2,1)S(1)} %get-tuple-element.185), channel_id=1, source_target_pairs={{0,2},{1,3},{2,0},{3,1},{4,6},{5,7},{6,4},{7,5},{8,10},{9,11},{10,... | collective-permute-start | bytes 294920 | tf_op jit(solution)/shard_map/ppermute | solution.py:56
  213.0 16.4 %collective-permute-start.71 = (bf16[128,768]{1,0:T(8,128)(2,1)S(1)}, bf16[128,768]{1,0:T(8,128)(2,1)S(1)}, u32[]{:S(2)}, u32[]{:S(2)}) collective-permute-start(bf16[128,768]{1,0:T(8,128)(2,1)S(1)} %get-tuple-element.200), channel_id=1, source_target_pairs={{0,4},{4,0},{8,12},{12,8},{1,5},{5,1},{9,13},{13,9},{2,6},{6,2},{1... | collective-permute-start | bytes 589832 | tf_op jit(solution)/shard_map/ppermute | solution.py:56
  214.0 15.4 %collective-permute-start.72 = (bf16[128,768]{1,0:T(8,128)(2,1)S(1)}, bf16[128,768]{1,0:T(8,128)(2,1)S(1)}, u32[]{:S(2)}, u32[]{:S(2)}) collective-permute-start(bf16[128,768]{1,0:T(8,128)(2,1)S(1)} %get-tuple-element.201), channel_id=1, source_target_pairs={{0,8},{4,12},{8,0},{12,4},{1,9},{5,13},{9,1},{13,5},{2,10},{6,14},... | collective-permute-start | bytes 589832 | tf_op jit(solution)/shard_map/ppermute | solution.py:56
  214.0 15.4 %collective-permute-start.73 = (bf16[128,768]{1,0:T(8,128)(2,1)S(1)}, bf16[128,768]{1,0:T(8,128)(2,1)S(1)}, u32[]{:S(2)}, u32[]{:S(2)}) collective-permute-start(bf16[128,768]{1,0:T(8,128)(2,1)S(1)} %get-tuple-element.202), channel_id=1, source_target_pairs={{0,12},{4,8},{8,4},{12,0},{1,13},{5,9},{9,5},{13,1},{2,14},{6,10},... | collective-permute-start | bytes 589832 | tf_op jit(solution)/shard_map/ppermute | solution.py:56
  231.8 19.2 %collective-permute-start.81 = (bf16[384,768]{1,0:T(8,128)(2,1)S(1)}, bf16[384,768]{1,0:T(8,128)(2,1)S(1)}, u32[]{:S(2)}, u32[]{:S(2)}) collective-permute-start(bf16[384,768]{1,0:T(8,128)(2,1)S(1)} %get-tuple-element.210.refs_12_), channel_id=1, source_target_pairs={{0,4},{4,0},{8,12},{12,8},{1,5},{5,1},{9,13},{13,9},{2,6},{6,2},{1... | collective-permute-start | bytes 1769480 | tf_op jit(solution)/shard_map/ppermute | solution.py:56
  232.8 18.2 %collective-permute-start.82 = (bf16[384,768]{1,0:T(8,128)(2,1)S(1)}, bf16[384,768]{1,0:T(8,128)(2,1)S(1)}, u32[]{:S(2)}, u32[]{:S(2)}) collective-permute-start(bf16[384,768]{1,0:T(8,128)(2,1)S(1)} %get-tuple-element.219), channel_id=1, source_target_pairs={{0,8},{4,12},{8,0},{12,4},{1,9},{5,13},{9,1},{13,5},{2,10},{6,14},... | collective-permute-start | bytes 1769480 | tf_op jit(solution)/shard_map/ppermute | solution.py:56
  247.9 13.3 %collective-permute-start.80 = (bf16[80,3072]{1,0:T(8,128)(2,1)S(1)}, bf16[80,3072]{1,0:T(8,128)(2,1)S(1)}, u32[]{:S(2)}, u32[]{:S(2)}) collective-permute-start(bf16[80,3072]{1,0:T(8,128)(2,1)S(1)} %get-tuple-element.216), channel_id=1, source_target_pairs={{0,16},{16,0},{1,17},{17,1},{2,18},{18,2},{3,19},{19,3},{4,20},{20... | collective-permute-start | bytes 1474568 | tf_op jit(solution)/shard_map/ppermute | solution.py:40
  263.9 16.4 %collective-permute-start.85 = (bf16[384,896]{1,0:T(8,128)(2,1)S(1)}, bf16[384,896]{1,0:T(8,128)(2,1)S(1)}, u32[]{:S(2)}, u32[]{:S(2)}) collective-permute-start(bf16[384,896]{1,0:T(8,128)(2,1)S(1)} %get-tuple-element.226.refs_5_), channel_id=1, source_target_pairs={{0,4},{4,0},{8,12},{12,8},{1,5},{5,1},{9,13},{13,9},{2,6},{6,2},{1... | collective-permute-start | bytes 2064392 | tf_op jit(solution)/shard_map/ppermute | solution.py:56
  264.6 20.9 %collective-permute-start.89 = (bf16[768,768]{1,0:T(8,128)(2,1)S(1)}, bf16[768,768]{1,0:T(8,128)(2,1)S(1)}, u32[]{:S(2)}, u32[]{:S(2)}) collective-permute-start(bf16[768,768]{1,0:T(8,128)(2,1)S(1)} %get-tuple-element.213.refs_13_), channel_id=1, source_target_pairs={{0,16},{16,0},{1,17},{17,1},{2,18},{18,2},{3,19},{19,3},{4,20},{20... | collective-permute-start | bytes 3538952 | tf_op jit(solution)/shard_map/ppermute | solution.py:40
  266.0 20.6 %collective-permute-start.90 = (bf16[768,768]{1,0:T(8,128)(2,1)S(1)}, bf16[768,768]{1,0:T(8,128)(2,1)S(1)}, u32[]{:S(2)}, u32[]{:S(2)}) collective-permute-start(bf16[768,768]{1,0:T(8,128)(2,1)S(1)} %get-tuple-element.234), channel_id=1, source_target_pairs={{0,16},{16,0},{1,17},{17,1},{2,18},{18,2},{3,19},{19,3},{4,20},{20... | collective-permute-start | bytes 3538952 | tf_op jit(solution)/shard_map/ppermute | solution.py:40
  266.0 14.4 %collective-permute-start.86 = (bf16[384,768]{1,0:T(8,128)(2,1)S(1)}, bf16[384,768]{1,0:T(8,128)(2,1)S(1)}, u32[]{:S(2)}, u32[]{:S(2)}) collective-permute-start(bf16[384,768]{1,0:T(8,128)(2,1)S(1)} %get-tuple-element.228), channel_id=1, source_target_pairs={{0,8},{4,12},{8,0},{12,4},{1,9},{5,13},{9,1},{13,5},{2,10},{6,14},... | collective-permute-start | bytes 1769480 | tf_op jit(solution)/shard_map/ppermute | solution.py:56
  280.7 11.1 %collective-permute-start.87 = (bf16[192,896]{1,0:T(8,128)(2,1)S(1)}, bf16[192,896]{1,0:T(8,128)(2,1)S(1)}, u32[]{:S(2)}, u32[]{:S(2)}) collective-permute-start(bf16[192,896]{1,0:T(8,128)(2,1)S(1)} %get-tuple-element.231), channel_id=1, source_target_pairs={{0,8},{4,12},{8,0},{12,4},{1,9},{5,13},{9,1},{13,5},{2,10},{6,14},... | collective-permute-start | bytes 1032200 | tf_op jit(solution)/shard_map/ppermute | solution.py:56
  284.1 12.6 %collective-permute-start.94 = (bf16[48,1536]{1,0:T(8,128)(2,1)S(1)}, bf16[48,1536]{1,0:T(8,128)(2,1)S(1)}, u32[]{:S(2)}, u32[]{:S(2)}) collective-permute-start(bf16[48,1536]{1,0:T(8,128)(2,1)S(1)} %get-tuple-element.240), channel_id=1, source_target_pairs={{0,1},{1,0},{2,3},{3,2},{4,5},{5,4},{6,7},{7,6},{8,9},{9,8},{10,11... | collective-permute-start | bytes 442376 | tf_op jit(solution)/shard_map/ppermute | solution.py:56
  285.4 12.4 %collective-permute-start.95 = (bf16[48,1536]{1,0:T(8,128)(2,1)S(1)}, bf16[48,1536]{1,0:T(8,128)(2,1)S(1)}, u32[]{:S(2)}, u32[]{:S(2)}) collective-permute-start(bf16[48,1536]{1,0:T(8,128)(2,1)S(1)} %get-tuple-element.241), channel_id=1, source_target_pairs={{0,2},{1,3},{2,0},{3,1},{4,6},{5,7},{6,4},{7,5},{8,10},{9,11},{10,... | collective-permute-start | bytes 442376 | tf_op jit(solution)/shard_map/ppermute | solution.py:56
  286.6 14.2 %collective-permute-start.96 = (bf16[48,1536]{1,0:T(8,128)(2,1)S(1)}, bf16[48,1536]{1,0:T(8,128)(2,1)S(1)}, u32[]{:S(2)}, u32[]{:S(2)}) collective-permute-start(bf16[48,1536]{1,0:T(8,128)(2,1)S(1)} %get-tuple-element.242), channel_id=1, source_target_pairs={{0,3},{1,2},{2,1},{3,0},{4,7},{5,6},{6,5},{7,4},{8,11},{9,10},{10,... | collective-permute-start | bytes 442376 | tf_op jit(solution)/shard_map/ppermute | solution.py:56
  294.2 8.8 %collective-permute-start.91 = (bf16[48,1664]{1,0:T(8,128)(2,1)S(1)}, bf16[48,1664]{1,0:T(8,128)(2,1)S(1)}, u32[]{:S(2)}, u32[]{:S(2)}) collective-permute-start(bf16[48,1664]{1,0:T(8,128)(2,1)S(1)} %get-tuple-element.237), channel_id=1, source_target_pairs={{0,1},{1,0},{2,3},{3,2},{4,5},{5,4},{6,7},{7,6},{8,9},{9,8},{10,11... | collective-permute-start | bytes 479240 | tf_op jit(solution)/shard_map/ppermute | solution.py:56
  295.5 15.5 %collective-permute-start.92 = (bf16[48,1664]{1,0:T(8,128)(2,1)S(1)}, bf16[48,1664]{1,0:T(8,128)(2,1)S(1)}, u32[]{:S(2)}, u32[]{:S(2)}) collective-permute-start(bf16[48,1664]{1,0:T(8,128)(2,1)S(1)} %get-tuple-element.238), channel_id=1, source_target_pairs={{0,2},{1,3},{2,0},{3,1},{4,6},{5,7},{6,4},{7,5},{8,10},{9,11},{10,... | collective-permute-start | bytes 479240 | tf_op jit(solution)/shard_map/ppermute | solution.py:56
  296.6 14.4 %collective-permute-start.93 = (bf16[48,1664]{1,0:T(8,128)(2,1)S(1)}, bf16[48,1664]{1,0:T(8,128)(2,1)S(1)}, u32[]{:S(2)}, u32[]{:S(2)}) collective-permute-start(bf16[48,1664]{1,0:T(8,128)(2,1)S(1)} %get-tuple-element.239), channel_id=1, source_target_pairs={{0,3},{1,2},{2,1},{3,0},{4,7},{5,6},{6,5},{7,4},{8,11},{9,10},{10,... | collective-permute-start | bytes 479240 | tf_op jit(solution)/shard_map/ppermute | solution.py:56
  297.8 17.0 %collective-permute-start.79 = (bf16[64,768]{1,0:T(8,128)(2,1)S(1)}, bf16[64,768]{1,0:T(8,128)(2,1)S(1)}, u32[]{:S(2)}, u32[]{:S(2)}) collective-permute-start(bf16[64,768]{1,0:T(8,128)(2,1)S(1)} %broadcast_select_fusion.1), channel_id=1, source_target_pairs={{0,16},{16,0},{1,17},{17,1},{2,18},{18,2},{3,19},{19,3},{4,20},{20... | collective-permute-start | bytes 294920 | tf_op jit(solution)/shard_map/ppermute | solution.py:40
  (60 other events, 395.6 us)
where the time goes:
time: 323 us; the launch traced here: 318 us
  starting transfers between devices  129 us (40%)
  waiting for transfers between devices  110 us (34%)
  Pallas kernels  69.6 us (22%)
  local copies, waits for them, and re-layouts  5.38 us (2%)
    ppermute x79, waiting for transfers between devices, hop(): return lax.ppermute(value, axis, [(i, i ^ step) for i in range(count)])  107 us
    ppermute x79, starting transfers between devices, hop(): return lax.ppermute(value, axis, [(i, i ^ step) for i in range(count)])  89.1 us
    pallas_call x35, Pallas kernels, call(): pl.pallas_call(run, out_shape=list(outs), in_specs=list(specs) + [AN] * l...  69.6 us
    ppermute x19, starting transfers between devices, swap(): return lax.ppermute(value, 'section', [(0, 1), (1, 0)])  40.2 us
  transfers between devices with their start and end apart: 98, of which 35 were waited for; matrix products, arithmetic and copies ran while one was open for 1% of the time, Pallas kernels for 13%

commit v1 on v0

--- a/solution.py
+++ b/solution.py
@@ -790,9 +790,10 @@
 def expert_weights(other, *refs):
     place, keeps, refs = refs[0], refs[1:3], refs[3:]
     if other:
-        in_ref, out_ref, held, sem = refs
+        both_ref, held, sem = refs
+        in_ref, out_ref = both_ref.at[0], both_ref.at[1]
     else:
-        came_in, came_out, in_ref, out_ref, held, sem = refs
+        came, in_ref, out_ref, held, sem = refs
     for layer in range(2):
 
         @pl.when((place[0] == layer) != other)
@@ -803,8 +804,8 @@
     grad_in = t_dot(held[0], held[1])
     grad_out = t_dot(held[2], held[3])
     if not other:
-        grad_in = grad_in + came_in[...].astype(F32)
-        grad_out = grad_out + came_out[...].astype(F32)
+        grad_in = grad_in + came[0].astype(F32)
+        grad_out = grad_out + came[1].astype(F32)
     in_ref[...] = grad_in.astype(in_ref.dtype)
     out_ref[...] = grad_out.astype(out_ref.dtype)
 
@@ -1159,7 +1160,7 @@
     keep_scratch = [pltpu.VMEM(keep_one.shape, BF), sems(())]
     sent = call(
         functools.partial(expert_weights, True),
-        [out(matrix)] * 2,
+        [out((2, *matrix))],
         [place, keep_zero, keep_one],
         [SM, HB, HB],
         keep_scratch,
@@ -1181,7 +1182,7 @@
         functools.partial(expert_weights, False),
         [out(matrix, F32)] * 2,
         [place, keep_zero, keep_one, *came_grads],
-        [SM, HB, HB, VM, VM],
+        [SM, HB, HB, VM],
         keep_scratch,
         after=blocks_zero[:1],
     )

time: 323 us -> 329 us (1.019)
  starting transfers between devices: 129 us -> 133 us
    ppermute x79, starting transfers between devices: 89.1 us -> 95.8 us  [hop(): return lax.ppermute(value, axis, [(i, i ^ step) for i in range(count)])]
    ppermute x19 -> x18, starting transfers between devices: 40.2 us -> 37.6 us  [swap(): return lax.ppermute(value, 'section', [(0, 1), (1, 0)])]
  transfers between devices with their start and end apart: 98 -> 97, of which waited for: 35 -> 38; matrix products, arithmetic and copies ran while one was open for 1% -> 1% of each run, Pallas kernels for 13% -> 14%
where the time goes in v1:
time: 329 us; the launch traced here: 323 us
  starting transfers between devices  133 us (40%)
  waiting for transfers between devices  111 us (34%)
  Pallas kernels  69.6 us (21%)
  local copies, waits for them, and re-layouts  5.38 us (2%)
    ppermute x79, waiting for transfers between devices, hop(): return lax.ppermute(value, axis, [(i, i ^ step) for i in range(count)])  110 us
    ppermute x79, starting transfers between devices, hop(): return lax.ppermute(value, axis, [(i, i ^ step) for i in range(count)])  95.8 us
    pallas_call x35, Pallas kernels, call(): pl.pallas_call(run, out_shape=list(outs), in_specs=list(specs) + [AN] * l...  69.6 us
    ppermute x18, starting transfers between devices, swap(): return lax.ppermute(value, 'section', [(0, 1), (1, 0)])  37.6 us
  transfers between devices with their start and end apart: 97, of which 38 were waited for; matrix products, arithmetic and copies ran while one was open for 1% of the time, Pallas kernels for 14%

profile of v1, /device:TPU:1, one launch (start us, length us, event | category | flops | bytes accessed | tf_op | source)
XLA Modules:
  0.0 323.5 jit_solution(6615067769991062823)
XLA Ops:
  1.8 2.5 shard_map.230
  6.0 4.5 %collective-permute-start.10 = (bf16[48,1664]{1,0:T(8,128)(2,1)S(1)}, bf16[48,1664]{1,0:T(8,128)(2,1)S(1)}, u32[]{:S(2)}, u32[]{:S(2)}) collective-permute-start(bf16[48,1664]{1,0:T(8,128)(2,1)S(1)} %broadcast_select_fusion.refs_1_), channel_id=1, source_target_pairs={{0,3},{1,2},{2,1},{3,0},{4,7},{5,6},{6,5},{7,4},{8,11},{9,10},{10,... | collective-permute-start | bytes 479240 | tf_op jit(solution)/shard_map/ppermute | solution.py:56
  15.6 2.9 collective-permute-done.8.refs_2_
  18.5 5.1 %collective-permute-done.9.refs_3_ = bf16[48,1664]{1,0:T(8,128)(2,1)S(1)} collective-permute-done((bf16[48,1664]{1,0:T(8,128)(2,1)S(1)}, bf16[48,1664]{1,0:T(8,128)(2,1)S(1)}, u32[]{:S(2)}, u32[]{:S(2)}) %collective-permute-start.9) | collective-permute-done | bytes 159776 | tf_op jit(solution)/shard_map/ppermute | solution.py:56
  30.9 7.8 %collective-permute-done.12.refs_6_.refs_4_ = bf16[192,1664]{1,0:T(8,128)(2,1)S(1)} collective-permute-done((bf16[192,1664]{1,0:T(8,128)(2,1)S(1)}, bf16[192,1664]{1,0:T(8,128)(2,1)S(1)}, u32[]{:S(2)}, u32[]{:S(2)}) %collective-permute-start.12) | collective-permute-done | bytes 639008 | tf_op jit(solution)/shard_map/ppermute | solution.py:56
  47.4 2.1 collective-permute-done.18.refs_3_
  50.7 3.1 collective-permute-done.19.refs_4_
  53.7 6.7 %collective-permute-start.22 = (bf16[192,1664]{1,0:T(8,128)(2,1)S(1)}, bf16[192,1664]{1,0:T(8,128)(2,1)S(1)}, u32[]{:S(2)}, u32[]{:S(2)}) collective-permute-start(bf16[192,1664]{1,0:T(8,128)(2,1)S(1)} %shard_map.232.refs_2_), channel_id=1, source_target_pairs={{0,16},{16,0},{1,17},{17,1},{2,18},{18,2},{3,19},{19,3},{4,20},{20... | collective-permute-start | bytes 1916936 | tf_op jit(solution)/shard_map/ppermute | solution.py:40
  61.0 2.8 collective-permute-start.25
  66.2 4.7 %shard_map.235 = (bf16[64,768]{1,0:T(8,128)(2,1)S(1)}, bf16[64,5376]{1,0:T(8,128)(2,1)S(1)}, f32[6,128,64]{2,1,0:T(8,128)S(1)}, f32[64,1024]{1,0:T(8,128)S(1)}, ...) custom-call(s32[10]{0:T(128)S(1)} %copy-done.4, s32[8,128]{1,0:T(8,128)S(1)} %get-tuple-element.130.refs_5_.refs_1_.refs_0_, ...), custom_call_target="tpu_custom_call" | custom-call | bytes 11767848 | tf_op jit(solution)/shard_map/pallas_call | solution.py:95
  75.5 3.1 collective-permute-done.29.refs_4_
  83.5 3.6 %collective-permute-done.31.refs_7_ = bf16[128,768]{1,0:T(8,128)(2,1)S(1)} collective-permute-done((bf16[128,768]{1,0:T(8,128)(2,1)S(1)}, bf16[128,768]{1,0:T(8,128)(2,1)S(1)}, u32[]{:S(2)}, u32[]{:S(2)}) %collective-permute-start.31) | collective-permute-done | bytes 196640 | tf_op jit(solution)/shard_map/ppermute | solution.py:56
  87.1 3.6 %shard_map.237 = (bf16[128,768]{1,0:T(8,128)(2,1)S(1)}, bf16[128,768]{1,0:T(8,128)(2,1)S(1)}, bf16[128,768]{1,0:T(8,128)(2,1)S(1)}, bf16[128,768]{1,0:T(8,128)(2,1)S(1)}, bf16[512,768]{1,0:T(8,128)(2,1)S(1)}) custom-call(s32[10]{0:T(128)S(1)} %copy-done.4, bf16[768,768]{1,0:T(8,128)(2,1)S(1)} %bitcast.37, bf16[768,768]{1,0:T(8,128)(2,1)S(1)} %bitcast.41, ...), custom_call_target="tpu_custom_call" | custom-call | bytes 7077928 | tf_op jit(solution)/shard_map/pallas_call | solution.py:95
  91.5 5.1 %collective-permute-start.33 = (bf16[768,1664]{1,0:T(8,128)(2,1)S(1)}, bf16[768,1664]{1,0:T(8,128)(2,1)S(1)}, u32[]{:S(2)}, u32[]{:S(2)}) collective-permute-start(bf16[768,1664]{1,0:T(8,128)(2,1)S(1)} %shard_map.238.refs_2_), channel_id=1, source_target_pairs={{0,16},{16,0},{1,17},{17,1},{2,18},{18,2},{3,19},{19,3},{4,20},{20... | collective-permute-start | bytes 7667720 | tf_op jit(solution)/shard_map/ppermute | solution.py:40
  99.3 2.8 collective-permute-start.46
  103.1 3.0 collective-permute-start.47
  108.3 2.4 collective-permute-start.37
  115.8 3.5 %collective-permute-done.38.refs_7_ = bf16[64,768]{1,0:T(8,128)(2,1)S(1)} collective-permute-done((bf16[64,768]{1,0:T(8,128)(2,1)S(1)}, bf16[64,768]{1,0:T(8,128)(2,1)S(1)}, u32[]{:S(2)}, u32[]{:S(2)}) %collective-permute-start.38) | collective-permute-done | bytes 98336 | tf_op jit(solution)/shard_map/ppermute | solution.py:56
  119.4 5.1 %shard_map.240 = (bf16[64,768]{1,0:T(8,128)(2,1)S(1)}, bf16[64,768]{1,0:T(8,128)(2,1)S(1)}, bf16[64,768]{1,0:T(8,128)(2,1)S(1)}, bf16[64,5376]{1,0:T(8,128)(2,1)...) custom-call(s32[10]{0:T(128)S(1)} %copy-done.4, ...), custom_call_target="tpu_custom_call" | custom-call | bytes 12521512 | tf_op jit(solution)/shard_map/pallas_call | solution.py:95
  124.5 3.5 %collective-permute-start.40 = (bf16[64,768]{1,0:T(8,128)(2,1)S(1)}, bf16[64,768]{1,0:T(8,128)(2,1)S(1)}, u32[]{:S(2)}, u32[]{:S(2)}) collective-permute-start(bf16[64,768]{1,0:T(8,128)(2,1)S(1)} %get-tuple-element.155.refs_1_), channel_id=1, source_target_pairs={{0,1},{1,0},{2,3},{3,2},{4,5},{5,4},{6,7},{7,6},{8,9},{9,8},{10,11... | collective-permute-start | bytes 294920 | tf_op jit(solution)/shard_map/ppermute | solution.py:56
  136.6 2.2 collective-permute-start.44
  140.9 7.7 %collective-permute-done.44.refs_8_ = bf16[128,768]{1,0:T(8,128)(2,1)S(1)} collective-permute-done((bf16[128,768]{1,0:T(8,128)(2,1)S(1)}, bf16[128,768]{1,0:T(8,128)(2,1)S(1)}, u32[]{:S(2)}, u32[]{:S(2)}) %collective-permute-start.44) | collective-permute-done | bytes 196640 | tf_op jit(solution)/shard_map/ppermute | solution.py:56
  148.6 11.2 %shard_map.243 = (bf16[128,768]{1,0:T(8,128)(2,1)S(1)}, bf16[128,768]{1,0:T(8,128)(2,1)S(1)}, bf16[128,768]{1,0:T(8,128)(2,1)S(1)}, bf16[128,768]{1,0:T(8,128)(2...) custom-call(s32[10]{0:T(128)S(1)} %copy-done.4, ...), custom_call_target="tpu_custom_call" | custom-call | bytes 11206696 | tf_op jit(solution)/shard_map/pallas_call | solution.py:95
  159.9 2.3 collective-permute-start.53
  166.5 4.8 %collective-permute-done.54.refs_4_ = bf16[128,768]{1,0:T(8,128)(2,1)S(1)} collective-permute-done((bf16[128,768]{1,0:T(8,128)(2,1)S(1)}, bf16[128,768]{1,0:T(8,128)(2,1)S(1)}, u32[]{:S(2)}, u32[]{:S(2)}) %collective-permute-start.54) | collective-permute-done | bytes 196640 | tf_op jit(solution)/shard_map/ppermute | solution.py:56
  171.8 2.6 collective-permute-start.60
  179.7 2.7 collective-permute-done.57.refs_10_
  182.4 5.9 %shard_map.246 = (bf16[64,768]{1,0:T(8,128)(2,1)S(1)}, bf16[80,3072]{1,0:T(8,128)(2,1)S(1)}, bf16[64,3072]{1,0:T(8,128)(2,1)S(1)}, f32[16,768]{1,0:T(8,128)S(1)}) custom-call(s32[10]{0:T(128)S(1)} %copy-done.4, s32[8,128]{1,0:T(8,128)S(1)} %get-tuple-element.130.refs_5_.refs_1_.refs_0_, bf16[2,768,1664]{2,1,0:T(8,128)(2,1)S(1)} %get-tuple-element.152.refs_2_, ...), custom_call_target="tpu_custom_call" | custom-call | bytes 7786536 | tf_op jit(solution)/shard_map/pallas_call | solution.py:95
  188.3 2.2 collective-permute-start.66
  191.9 6.0 %collective-permute-start.78 = (bf16[80,3072]{1,0:T(8,128)(2,1)S(1)}, bf16[80,3072]{1,0:T(8,128)(2,1)S(1)}, u32[]{:S(2)}, u32[]{:S(2)}) collective-permute-start(bf16[80,3072]{1,0:T(8,128)(2,1)S(1)} %get-tuple-element.207), channel_id=1, source_target_pairs={{0,16},{16,0},{1,17},{17,1},{2,18},{18,2},{3,19},{19,3},{4,20},{20... | collective-permute-start | bytes 1474568 | tf_op jit(solution)/shard_map/ppermute | solution.py:40
  202.7 4.6 %collective-permute-start.63 = (bf16[64,768]{1,0:T(8,128)(2,1)S(1)}, bf16[64,768]{1,0:T(8,128)(2,1)S(1)}, u32[]{:S(2)}, u32[]{:S(2)}) collective-permute-start(bf16[64,768]{1,0:T(8,128)(2,1)S(1)} %get-tuple-element.184), channel_id=1, source_target_pairs={{0,3},{1,2},{2,1},{3,0},{4,7},{5,6},{6,5},{7,4},{8,11},{9,10},{10,... | collective-permute-start | bytes 294920 | tf_op jit(solution)/shard_map/ppermute | solution.py:56
  209.9 3.8 %collective-permute-start.74 = (f32[16,768]{1,0:T(8,128)S(1)}, f32[16,768]{1,0:T(8,128)S(1)}, u32[]{:S(2)}, u32[]{:S(2)}) collective-permute-start(f32[16,768]{1,0:T(8,128)S(1)} %get-tuple-element.201.refs_4_), channel_id=1, source_target_pairs={{0,16},{16,0},{1,17},{17,1},{2,18},{18,2},{3,19},{19,3},{4,20},{20... | collective-permute-start | bytes 147464 | tf_op jit(solution)/shard_map/ppermute | solution.py:40
  213.7 7.4 %shard_map.249 = (bf16[128,768]{1,0:T(8,128)(2,1)S(1)}, bf16[128,768]{1,0:T(8,128)(2,1)S(1)}, bf16[128,768]{1,0:T(8,128)(2,1)S(1)}, bf16[128,768]{1,0:T(8,128)(2,1)S(1)}, bf16[4,512,768]{2,1,0:T(8,128)(2,1)S(1)}) custom-call(s32[10]{0:T(128)S(1)} %copy-done.4, bf16[768,768]{1,0:T(8,128)(2,1)S(1)} %bitcast.39, bf16[768,768]{1,0:T(8,128)(2,1)S(1)} %bitcast.43, ...), custom_call_target="tpu_custom_call" | custom-call | bytes 10420264 | tf_op jit(solution)/shard_map/pallas_call | solution.py:95
  221.0 2.2 shard_map.252.refs_13_
  226.0 3.4 %collective-permute-done.71.refs_2_ = bf16[128,768]{1,0:T(8,128)(2,1)S(1)} collective-permute-done((bf16[128,768]{1,0:T(8,128)(2,1)S(1)}, bf16[128,768]{1,0:T(8,128)(2,1)S(1)}, u32[]{:S(2)}, u32[]{:S(2)}) %collective-permute-start.71) | collective-permute-done | bytes 196640 | tf_op jit(solution)/shard_map/ppermute | solution.py:56
  229.7 4.0 %collective-permute-done.73.refs_4_ = bf16[128,768]{1,0:T(8,128)(2,1)S(1)} collective-permute-done((bf16[128,768]{1,0:T(8,128)(2,1)S(1)}, bf16[128,768]{1,0:T(8,128)(2,1)S(1)}, u32[]{:S(2)}, u32[]{:S(2)}) %collective-permute-start.73) | collective-permute-done | bytes 196640 | tf_op jit(solution)/shard_map/ppermute | solution.py:56
  234.0 2.1 shard_map.251
  241.6 2.2 collective-permute-start.77
  244.5 2.7 collective-permute-done.77.refs_11_
  247.2 5.8 %shard_map.253 = (bf16[64,768]{1,0:T(8,128)(2,1)S(1)}, bf16[80,3072]{1,0:T(8,128)(2,1)S(1)}, bf16[64,3072]{1,0:T(8,128)(2,1)S(1)}, f32[16,768]{1,0:T(8,128)S(1)}) custom-call(s32[10]{0:T(128)S(1)} %copy-done.4, s32[8,128]{1,0:T(8,128)S(1)} %get-tuple-element.130.refs_5_.refs_1_.refs_0_, bf16[2,768,1664]{2,1,0:T(8,128)(2,1)S(1)} %get-tuple-element.186.refs_2_, ...), custom_call_target="tpu_custom_call" | custom-call | bytes 7884840 | tf_op jit(solution)/shard_map/pallas_call | solution.py:95
  253.0 4.7 %collective-permute-start.80 = (bf16[80,3072]{1,0:T(8,128)(2,1)S(1)}, bf16[80,3072]{1,0:T(8,128)(2,1)S(1)}, u32[]{:S(2)}, u32[]{:S(2)}) collective-permute-start(bf16[80,3072]{1,0:T(8,128)(2,1)S(1)} %get-tuple-element.213), channel_id=1, source_target_pairs={{0,16},{16,0},{1,17},{17,1},{2,18},{18,2},{3,19},{19,3},{4,20},{20... | collective-permute-start | bytes 1474568 | tf_op jit(solution)/shard_map/ppermute | solution.py:40
  259.7 7.0 %collective-permute-done.83.refs_2_ = bf16[192,768]{1,0:T(8,128)(2,1)S(1)} collective-permute-done((bf16[192,768]{1,0:T(8,128)(2,1)S(1)}, bf16[192,768]{1,0:T(8,128)(2,1)S(1)}, u32[]{:S(2)}, u32[]{:S(2)}) %collective-permute-start.83) | collective-permute-done | bytes 294944 | tf_op jit(solution)/shard_map/ppermute | solution.py:56
  268.0 2.7 shard_map.256
  271.9 13.0 %collective-permute-done.86.refs_2_ = bf16[384,768]{1,0:T(8,128)(2,1)S(1)} collective-permute-done((bf16[384,768]{1,0:T(8,128)(2,1)S(1)}, bf16[384,768]{1,0:T(8,128)(2,1)S(1)}, u32[]{:S(2)}, u32[]{:S(2)}) %collective-permute-start.86) | collective-permute-done | bytes 589856 | tf_op jit(solution)/shard_map/ppermute | solution.py:56
  287.5 2.4 collective-permute-start.64
  294.1 4.0 %shard_map.258 = (f32[768,768]{1,0:T(8,128)}, f32[768,768]{1,0:T(8,128)}) custom-call(s32[10]{0:T(128)S(1)} %copy-done.5, bf16[4,512,768]{2,1,0:T(8,128)(2,1)S(1)} %get-tuple-element.209.refs_1_, bf16[4,512,768]{2,1,0:T(8,128)(2,1)S(1)} %get-tuple-element.210.refs_2_, bf16[2,768,768]{2,1,0:T(8,128)(2,1)S(1)} %collective-permute-done.89.refs_3_, ...), custom_call_target="tpu_custom_call" | custom-call | bytes 13369384 | tf_op jit(solution)/shard_map/pallas_call | solution.py:95
  307.6 9.1 %collective-permute-done.91.refs_3_ = bf16[48,1664]{1,0:T(8,128)(2,1)S(1)} collective-permute-done((bf16[48,1664]{1,0:T(8,128)(2,1)S(1)}, bf16[48,1664]{1,0:T(8,128)(2,1)S(1)}, u32[]{:S(2)}, u32[]{:S(2)}) %collective-permute-start.91) | collective-permute-done | bytes 159776 | tf_op jit(solution)/shard_map/ppermute | solution.py:56
  317.9 2.5 collective-permute-start.96
  (214 shorter events, 112.8 us)
Async XLA Ops:
  0.6 10.5 %collective-permute-start.2 = (bf16[768,768]{1,0:T(8,128)(2,1)}, bf16[768,768]{1,0:T(8,128)(2,1)S(1)}, u32[]{:S(2)}, u32[]{:S(2)}) collective-permute-start(bf16[768,768]{1,0:T(8,128)(2,1)} %bitcast.36), channel_id=1, source_target_pairs={{0,16},{16,0},{1,17},{17,1},{2,18},{18,2},{3,19},{19,3},{4,20},{20... | collective-permute-start | bytes 3538952 | tf_op jit(solution)/shard_map/ppermute | solution.py:40
  0.8 10.4 %collective-permute-start.3 = (bf16[768,768]{1,0:T(8,128)(2,1)}, bf16[768,768]{1,0:T(8,128)(2,1)S(1)}, u32[]{:S(2)}, u32[]{:S(2)}) collective-permute-start(bf16[768,768]{1,0:T(8,128)(2,1)} %bitcast.40), channel_id=1, source_target_pairs={{0,16},{16,0},{1,17},{17,1},{2,18},{18,2},{3,19},{19,3},{4,20},{20... | collective-permute-start | bytes 3538952 | tf_op jit(solution)/shard_map/ppermute | solution.py:40
  6.0 9.6 %collective-permute-start.10 = (bf16[48,1664]{1,0:T(8,128)(2,1)S(1)}, bf16[48,1664]{1,0:T(8,128)(2,1)S(1)}, u32[]{:S(2)}, u32[]{:S(2)}) collective-permute-start(bf16[48,1664]{1,0:T(8,128)(2,1)S(1)} %broadcast_select_fusion.refs_1_), channel_id=1, source_target_pairs={{0,3},{1,2},{2,1},{3,0},{4,7},{5,6},{6,5},{7,4},{8,11},{9,10},{10,... | collective-permute-start | bytes 479240 | tf_op jit(solution)/shard_map/ppermute | solution.py:56
  10.6 13.1 %collective-permute-start.9 = (bf16[48,1664]{1,0:T(8,128)(2,1)S(1)}, bf16[48,1664]{1,0:T(8,128)(2,1)S(1)}, u32[]{:S(2)}, u32[]{:S(2)}) collective-permute-start(bf16[48,1664]{1,0:T(8,128)(2,1)S(1)} %broadcast_select_fusion.refs_1_), channel_id=1, source_target_pairs={{0,2},{1,3},{2,0},{3,1},{4,6},{5,7},{6,4},{7,5},{8,10},{9,11},{10,... | collective-permute-start | bytes 479240 | tf_op jit(solution)/shard_map/ppermute | solution.py:56
  24.2 14.5 %collective-permute-start.12 = (bf16[192,1664]{1,0:T(8,128)(2,1)S(1)}, bf16[192,1664]{1,0:T(8,128)(2,1)S(1)}, u32[]{:S(2)}, u32[]{:S(2)}) collective-permute-start(bf16[192,1664]{1,0:T(8,128)(2,1)S(1)} %shard_map.232.refs_2_), channel_id=1, source_target_pairs={{0,8},{4,12},{8,0},{12,4},{1,9},{5,13},{9,1},{13,5},{2,10},{6,14},... | collective-permute-start | bytes 1916936 | tf_op jit(solution)/shard_map/ppermute | solution.py:56
  25.5 14.5 %collective-permute-start.11 = (bf16[192,1664]{1,0:T(8,128)(2,1)S(1)}, bf16[192,1664]{1,0:T(8,128)(2,1)S(1)}, u32[]{:S(2)}, u32[]{:S(2)}) collective-permute-start(bf16[192,1664]{1,0:T(8,128)(2,1)S(1)} %shard_map.232.refs_2_), channel_id=1, source_target_pairs={{0,4},{4,0},{8,12},{12,8},{1,5},{5,1},{9,13},{13,9},{2,6},{6,2},{1... | collective-permute-start | bytes 1916936 | tf_op jit(solution)/shard_map/ppermute | solution.py:56
  27.3 14.1 %collective-permute-start.5 = (bf16[48,1664]{1,0:T(8,128)(2,1)S(1)}, bf16[48,1664]{1,0:T(8,128)(2,1)S(1)}, u32[]{:S(2)}, u32[]{:S(2)}) collective-permute-start(bf16[48,1664]{1,0:T(8,128)(2,1)S(1)} %shard_map.231.refs_1_), channel_id=1, source_target_pairs={{0,1},{1,0},{2,3},{3,2},{4,5},{5,4},{6,7},{7,6},{8,9},{9,8},{10,11... | collective-permute-start | bytes 479240 | tf_op jit(solution)/shard_map/ppermute | solution.py:56
  27.4 14.0 %collective-permute-start.6 = (bf16[48,1664]{1,0:T(8,128)(2,1)S(1)}, bf16[48,1664]{1,0:T(8,128)(2,1)S(1)}, u32[]{:S(2)}, u32[]{:S(2)}) collective-permute-start(bf16[48,1664]{1,0:T(8,128)(2,1)S(1)} %shard_map.231.refs_1_), channel_id=1, source_target_pairs={{0,2},{1,3},{2,0},{3,1},{4,6},{5,7},{6,4},{7,5},{8,10},{9,11},{10,... | collective-permute-start | bytes 479240 | tf_op jit(solution)/shard_map/ppermute | solution.py:56
  29.5 11.9 %collective-permute-start.7 = (bf16[48,1664]{1,0:T(8,128)(2,1)S(1)}, bf16[48,1664]{1,0:T(8,128)(2,1)S(1)}, u32[]{:S(2)}, u32[]{:S(2)}) collective-permute-start(bf16[48,1664]{1,0:T(8,128)(2,1)S(1)} %shard_map.231.refs_1_), channel_id=1, source_target_pairs={{0,3},{1,2},{2,1},{3,0},{4,7},{5,6},{6,5},{7,4},{8,11},{9,10},{10,... | collective-permute-start | bytes 479240 | tf_op jit(solution)/shard_map/ppermute | solution.py:56
  38.8 21.7 %collective-permute-start.20 = (bf16[96,1664]{1,0:T(8,128)(2,1)S(1)}, bf16[96,1664]{1,0:T(8,128)(2,1)S(1)}, u32[]{:S(2)}, u32[]{:S(2)}) collective-permute-start(bf16[96,1664]{1,0:T(8,128)(2,1)S(1)} %slice.18), channel_id=1, source_target_pairs={{0,4},{4,0},{8,12},{12,8},{1,5},{5,1},{9,13},{13,9},{2,6},{6,2},{1... | collective-permute-start | bytes 958472 | tf_op jit(solution)/shard_map/ppermute | solution.py:56
  40.1 20.4 %collective-permute-start.21 = (bf16[96,1664]{1,0:T(8,128)(2,1)S(1)}, bf16[96,1664]{1,0:T(8,128)(2,1)S(1)}, u32[]{:S(2)}, u32[]{:S(2)}) collective-permute-start(bf16[96,1664]{1,0:T(8,128)(2,1)S(1)} %slice.19), channel_id=1, source_target_pairs={{0,8},{4,12},{8,0},{12,4},{1,9},{5,13},{9,1},{13,5},{2,10},{6,14},... | collective-permute-start | bytes 958472 | tf_op jit(solution)/shard_map/ppermute | solution.py:56
  42.0 19.0 %collective-permute-start.14 = (bf16[192,1664]{1,0:T(8,128)(2,1)S(1)}, bf16[192,1664]{1,0:T(8,128)(2,1)S(1)}, u32[]{:S(2)}, u32[]{:S(2)}) collective-permute-start(bf16[192,1664]{1,0:T(8,128)(2,1)S(1)} %shard_map.233.refs_1_), channel_id=1, source_target_pairs={{0,8},{4,12},{8,0},{12,4},{1,9},{5,13},{9,1},{13,5},{2,10},{6,14},... | collective-permute-start | bytes 1916936 | tf_op jit(solution)/shard_map/ppermute | solution.py:56
  42.3 21.5 %collective-permute-start.13 = (bf16[192,1664]{1,0:T(8,128)(2,1)S(1)}, bf16[192,1664]{1,0:T(8,128)(2,1)S(1)}, u32[]{:S(2)}, u32[]{:S(2)}) collective-permute-start(bf16[192,1664]{1,0:T(8,128)(2,1)S(1)} %shard_map.233.refs_1_), channel_id=1, source_target_pairs={{0,4},{4,0},{8,12},{12,8},{1,5},{5,1},{9,13},{13,9},{2,6},{6,2},{1... | collective-permute-start | bytes 1916936 | tf_op jit(solution)/shard_map/ppermute | solution.py:56
  53.7 10.1 %collective-permute-start.22 = (bf16[192,1664]{1,0:T(8,128)(2,1)S(1)}, bf16[192,1664]{1,0:T(8,128)(2,1)S(1)}, u32[]{:S(2)}, u32[]{:S(2)}) collective-permute-start(bf16[192,1664]{1,0:T(8,128)(2,1)S(1)} %shard_map.232.refs_2_), channel_id=1, source_target_pairs={{0,16},{16,0},{1,17},{17,1},{2,18},{18,2},{3,19},{19,3},{4,20},{20... | collective-permute-start | bytes 1916936 | tf_op jit(solution)/shard_map/ppermute | solution.py:40
  63.9 23.2 %collective-permute-start.15 = (bf16[96,1664]{1,0:T(8,128)(2,1)S(1)}, bf16[96,1664]{1,0:T(8,128)(2,1)S(1)}, u32[]{:S(2)}, u32[]{:S(2)}) collective-permute-start(bf16[96,1664]{1,0:T(8,128)(2,1)S(1)} %slice.16), channel_id=1, source_target_pairs={{0,4},{4,0},{8,12},{12,8},{1,5},{5,1},{9,13},{13,9},{2,6},{6,2},{1... | collective-permute-start | bytes 958472 | tf_op jit(solution)/shard_map/ppermute | solution.py:56
  64.8 22.3 %collective-permute-start.16 = (bf16[96,1664]{1,0:T(8,128)(2,1)S(1)}, bf16[96,1664]{1,0:T(8,128)(2,1)S(1)}, u32[]{:S(2)}, u32[]{:S(2)}) collective-permute-start(bf16[96,1664]{1,0:T(8,128)(2,1)S(1)} %slice.17), channel_id=1, source_target_pairs={{0,8},{4,12},{8,0},{12,4},{1,9},{5,13},{9,1},{13,5},{2,10},{6,14},... | collective-permute-start | bytes 958472 | tf_op jit(solution)/shard_map/ppermute | solution.py:56
  91.5 27.9 %collective-permute-start.33 = (bf16[768,1664]{1,0:T(8,128)(2,1)S(1)}, bf16[768,1664]{1,0:T(8,128)(2,1)S(1)}, u32[]{:S(2)}, u32[]{:S(2)}) collective-permute-start(bf16[768,1664]{1,0:T(8,128)(2,1)S(1)} %shard_map.238.refs_2_), channel_id=1, source_target_pairs={{0,16},{16,0},{1,17},{17,1},{2,18},{18,2},{3,19},{19,3},{4,20},{20... | collective-permute-start | bytes 7667720 | tf_op jit(solution)/shard_map/ppermute | solution.py:40
  96.9 9.2 %collective-permute-start.35 = (bf16[128,768]{1,0:T(8,128)(2,1)S(1)}, bf16[128,768]{1,0:T(8,128)(2,1)S(1)}, u32[]{:S(2)}, u32[]{:S(2)}) collective-permute-start(bf16[128,768]{1,0:T(8,128)(2,1)S(1)} %get-tuple-element.142), channel_id=1, source_target_pairs={{0,8},{4,12},{8,0},{12,4},{1,9},{5,13},{9,1},{13,5},{2,10},{6,14},... | collective-permute-start | bytes 589832 | tf_op jit(solution)/shard_map/ppermute | solution.py:56
  97.7 10.3 %collective-permute-start.36 = (bf16[128,768]{1,0:T(8,128)(2,1)S(1)}, bf16[128,768]{1,0:T(8,128)(2,1)S(1)}, u32[]{:S(2)}, u32[]{:S(2)}) collective-permute-start(bf16[128,768]{1,0:T(8,128)(2,1)S(1)} %get-tuple-element.143), channel_id=1, source_target_pairs={{0,12},{4,8},{8,4},{12,0},{1,13},{5,9},{9,5},{13,1},{2,14},{6,10},... | collective-permute-start | bytes 589832 | tf_op jit(solution)/shard_map/ppermute | solution.py:56
  99.3 11.5 %collective-permute-start.46 = (bf16[64,768]{1,0:T(8,128)(2,1)S(1)}, bf16[64,768]{1,0:T(8,128)(2,1)S(1)}, u32[]{:S(2)}, u32[]{:S(2)}) collective-permute-start(bf16[64,768]{1,0:T(8,128)(2,1)S(1)} %get-tuple-element.149.refs_1_.refs_3_), channel_id=1, source_target_pairs={{0,1},{1,0},{2,3},{3,2},{4,5},{5,4},{6,7},{7,6},{8,9},{9,8},{10,11... | collective-permute-start | bytes 294920 | tf_op jit(solution)/shard_map/ppermute | solution.py:56
  113.3 25.6 %collective-permute-start.49 = (bf16[128,768]{1,0:T(8,128)(2,1)S(1)}, bf16[128,768]{1,0:T(8,128)(2,1)S(1)}, u32[]{:S(2)}, u32[]{:S(2)}) collective-permute-start(bf16[128,768]{1,0:T(8,128)(2,1)S(1)} %get-tuple-element.161), channel_id=1, source_target_pairs={{0,4},{4,0},{8,12},{12,8},{1,5},{5,1},{9,13},{13,9},{2,6},{6,2},{1... | collective-permute-start | bytes 589832 | tf_op jit(solution)/shard_map/ppermute | solution.py:56
  130.2 9.8 %collective-permute-start.50 = (bf16[128,768]{1,0:T(8,128)(2,1)S(1)}, bf16[128,768]{1,0:T(8,128)(2,1)S(1)}, u32[]{:S(2)}, u32[]{:S(2)}) collective-permute-start(bf16[128,768]{1,0:T(8,128)(2,1)S(1)} %get-tuple-element.162), channel_id=1, source_target_pairs={{0,8},{4,12},{8,0},{12,4},{1,9},{5,13},{9,1},{13,5},{2,10},{6,14},... | collective-permute-start | bytes 589832 | tf_op jit(solution)/shard_map/ppermute | solution.py:56
  131.3 8.7 %collective-permute-start.51 = (bf16[128,768]{1,0:T(8,128)(2,1)S(1)}, bf16[128,768]{1,0:T(8,128)(2,1)S(1)}, u32[]{:S(2)}, u32[]{:S(2)}) collective-permute-start(bf16[128,768]{1,0:T(8,128)(2,1)S(1)} %get-tuple-element.163), channel_id=1, source_target_pairs={{0,12},{4,8},{8,4},{12,0},{1,13},{5,9},{9,5},{13,1},{2,14},{6,10},... | collective-permute-start | bytes 589832 | tf_op jit(solution)/shard_map/ppermute | solution.py:56
  136.6 12.0 %collective-permute-start.44 = (bf16[128,768]{1,0:T(8,128)(2,1)S(1)}, bf16[128,768]{1,0:T(8,128)(2,1)S(1)}, u32[]{:S(2)}, u32[]{:S(2)}) collective-permute-start(bf16[128,768]{1,0:T(8,128)(2,1)S(1)} %get-tuple-element.158), channel_id=1, source_target_pairs={{0,8},{4,12},{8,0},{12,4},{1,9},{5,13},{9,1},{13,5},{2,10},{6,14},... | collective-permute-start | bytes 589832 | tf_op jit(solution)/shard_map/ppermute | solution.py:56
  138.9 9.8 %collective-permute-start.45 = (bf16[128,768]{1,0:T(8,128)(2,1)S(1)}, bf16[128,768]{1,0:T(8,128)(2,1)S(1)}, u32[]{:S(2)}, u32[]{:S(2)}) collective-permute-start(bf16[128,768]{1,0:T(8,128)(2,1)S(1)} %get-tuple-element.159), channel_id=1, source_target_pairs={{0,12},{4,8},{8,4},{12,0},{1,13},{5,9},{9,5},{13,1},{2,14},{6,10},... | collective-permute-start | bytes 589832 | tf_op jit(solution)/shard_map/ppermute | solution.py:56
  162.2 9.1 %collective-permute-start.54 = (bf16[128,768]{1,0:T(8,128)(2,1)S(1)}, bf16[128,768]{1,0:T(8,128)(2,1)S(1)}, u32[]{:S(2)}, u32[]{:S(2)}) collective-permute-start(bf16[128,768]{1,0:T(8,128)(2,1)S(1)} %get-tuple-element.167), channel_id=1, source_target_pairs={{0,12},{4,8},{8,4},{12,0},{1,13},{5,9},{9,5},{13,1},{2,14},{6,10},... | collective-permute-start | bytes 589832 | tf_op jit(solution)/shard_map/ppermute | solution.py:56
  188.3 9.6 %collective-permute-start.65 = (bf16[64,768]{1,0:T(8,128)(2,1)S(1)}, bf16[64,768]{1,0:T(8,128)(2,1)S(1)}, u32[]{:S(2)}, u32[]{:S(2)}) collective-permute-start(bf16[64,768]{1,0:T(8,128)(2,1)S(1)} %get-tuple-element.187.refs_1_.refs_3_), channel_id=1, source_target_pairs={{0,1},{1,0},{2,3},{3,2},{4,5},{5,4},{6,7},{7,6},{8,9},{9,8},{10,11... | collective-permute-start | bytes 294920 | tf_op jit(solution)/shard_map/ppermute | solution.py:56
  188.3 10.6 %collective-permute-start.66 = (bf16[64,768]{1,0:T(8,128)(2,1)S(1)}, bf16[64,768]{1,0:T(8,128)(2,1)S(1)}, u32[]{:S(2)}, u32[]{:S(2)}) collective-permute-start(bf16[64,768]{1,0:T(8,128)(2,1)S(1)} %get-tuple-element.187.refs_1_.refs_3_), channel_id=1, source_target_pairs={{0,2},{1,3},{2,0},{3,1},{4,6},{5,7},{6,4},{7,5},{8,10},{9,11},{10,... | collective-permute-start | bytes 294920 | tf_op jit(solution)/shard_map/ppermute | solution.py:56
  191.9 8.9 %collective-permute-start.61 = (bf16[64,768]{1,0:T(8,128)(2,1)S(1)}, bf16[64,768]{1,0:T(8,128)(2,1)S(1)}, u32[]{:S(2)}, u32[]{:S(2)}) collective-permute-start(bf16[64,768]{1,0:T(8,128)(2,1)S(1)} %get-tuple-element.182), channel_id=1, source_target_pairs={{0,1},{1,0},{2,3},{3,2},{4,5},{5,4},{6,7},{7,6},{8,9},{9,8},{10,11... | collective-permute-start | bytes 294920 | tf_op jit(solution)/shard_map/ppermute | solution.py:56
  191.9 42.1 %collective-permute-start.78 = (bf16[80,3072]{1,0:T(8,128)(2,1)S(1)}, bf16[80,3072]{1,0:T(8,128)(2,1)S(1)}, u32[]{:S(2)}, u32[]{:S(2)}) collective-permute-start(bf16[80,3072]{1,0:T(8,128)(2,1)S(1)} %get-tuple-element.207), channel_id=1, source_target_pairs={{0,16},{16,0},{1,17},{17,1},{2,18},{18,2},{3,19},{19,3},{4,20},{20... | collective-permute-start | bytes 1474568 | tf_op jit(solution)/shard_map/ppermute | solution.py:40
  199.3 14.4 %collective-permute-start.68 = (bf16[128,768]{1,0:T(8,128)(2,1)S(1)}, bf16[128,768]{1,0:T(8,128)(2,1)S(1)}, u32[]{:S(2)}, u32[]{:S(2)}) collective-permute-start(bf16[128,768]{1,0:T(8,128)(2,1)S(1)} %get-tuple-element.194), channel_id=1, source_target_pairs={{0,4},{4,0},{8,12},{12,8},{1,5},{5,1},{9,13},{13,9},{2,6},{6,2},{1... | collective-permute-start | bytes 589832 | tf_op jit(solution)/shard_map/ppermute | solution.py:56
  199.4 14.2 %collective-permute-start.69 = (bf16[128,768]{1,0:T(8,128)(2,1)S(1)}, bf16[128,768]{1,0:T(8,128)(2,1)S(1)}, u32[]{:S(2)}, u32[]{:S(2)}) collective-permute-start(bf16[128,768]{1,0:T(8,128)(2,1)S(1)} %get-tuple-element.195), channel_id=1, source_target_pairs={{0,8},{4,12},{8,0},{12,4},{1,9},{5,13},{9,1},{13,5},{2,10},{6,14},... | collective-permute-start | bytes 589832 | tf_op jit(solution)/shard_map/ppermute | solution.py:56
  200.8 12.8 %collective-permute-start.70 = (bf16[128,768]{1,0:T(8,128)(2,1)S(1)}, bf16[128,768]{1,0:T(8,128)(2,1)S(1)}, u32[]{:S(2)}, u32[]{:S(2)}) collective-permute-start(bf16[128,768]{1,0:T(8,128)(2,1)S(1)} %get-tuple-element.196), channel_id=1, source_target_pairs={{0,12},{4,8},{8,4},{12,0},{1,13},{5,9},{9,5},{13,1},{2,14},{6,10},... | collective-permute-start | bytes 589832 | tf_op jit(solution)/shard_map/ppermute | solution.py:56
  209.9 14.6 %collective-permute-start.74 = (f32[16,768]{1,0:T(8,128)S(1)}, f32[16,768]{1,0:T(8,128)S(1)}, u32[]{:S(2)}, u32[]{:S(2)}) collective-permute-start(f32[16,768]{1,0:T(8,128)S(1)} %get-tuple-element.201.refs_4_), channel_id=1, source_target_pairs={{0,16},{16,0},{1,17},{17,1},{2,18},{18,2},{3,19},{19,3},{4,20},{20... | collective-permute-start | bytes 147464 | tf_op jit(solution)/shard_map/ppermute | solution.py:40
  223.2 68.8 %collective-permute-start.89 = (bf16[2,768,768]{2,1,0:T(8,128)(2,1)S(1)}, bf16[2,768,768]{2,1,0:T(8,128)(2,1)S(1)}, u32[]{:S(2)}, u32[]{:S(2)}) collective-permute-start(bf16[2,768,768]{2,1,0:T(8,128)(2,1)S(1)} %shard_map.252.refs_13_), channel_id=1, source_target_pairs={{0,16},{16,0},{1,17},{17,1},{2,18},{18,2},{3,19},{19,3},{4,20},{20... | collective-permute-start | bytes 7077896 | tf_op jit(solution)/shard_map/ppermute | solution.py:40
  224.5 9.2 %collective-permute-start.73 = (bf16[128,768]{1,0:T(8,128)(2,1)S(1)}, bf16[128,768]{1,0:T(8,128)(2,1)S(1)}, u32[]{:S(2)}, u32[]{:S(2)}) collective-permute-start(bf16[128,768]{1,0:T(8,128)(2,1)S(1)} %get-tuple-element.200), channel_id=1, source_target_pairs={{0,12},{4,8},{8,4},{12,0},{1,13},{5,9},{9,5},{13,1},{2,14},{6,10},... | collective-permute-start | bytes 589832 | tf_op jit(solution)/shard_map/ppermute | solution.py:56
  236.1 21.6 %collective-permute-start.81 = (bf16[384,768]{1,0:T(8,128)(2,1)S(1)}, bf16[384,768]{1,0:T(8,128)(2,1)S(1)}, u32[]{:S(2)}, u32[]{:S(2)}) collective-permute-start(bf16[384,768]{1,0:T(8,128)(2,1)S(1)} %get-tuple-element.208.refs_12_), channel_id=1, source_target_pairs={{0,4},{4,0},{8,12},{12,8},{1,5},{5,1},{9,13},{13,9},{2,6},{6,2},{1... | collective-permute-start | bytes 1769480 | tf_op jit(solution)/shard_map/ppermute | solution.py:56
  237.0 20.7 %collective-permute-start.82 = (bf16[384,768]{1,0:T(8,128)(2,1)S(1)}, bf16[384,768]{1,0:T(8,128)(2,1)S(1)}, u32[]{:S(2)}, u32[]{:S(2)}) collective-permute-start(bf16[384,768]{1,0:T(8,128)(2,1)S(1)} %get-tuple-element.216), channel_id=1, source_target_pairs={{0,8},{4,12},{8,0},{12,4},{1,9},{5,13},{9,1},{13,5},{2,10},{6,14},... | collective-permute-start | bytes 1769480 | tf_op jit(solution)/shard_map/ppermute | solution.py:56
  253.0 15.0 %collective-permute-start.80 = (bf16[80,3072]{1,0:T(8,128)(2,1)S(1)}, bf16[80,3072]{1,0:T(8,128)(2,1)S(1)}, u32[]{:S(2)}, u32[]{:S(2)}) collective-permute-start(bf16[80,3072]{1,0:T(8,128)(2,1)S(1)} %get-tuple-element.213), channel_id=1, source_target_pairs={{0,16},{16,0},{1,17},{17,1},{2,18},{18,2},{3,19},{19,3},{4,20},{20... | collective-permute-start | bytes 1474568 | tf_op jit(solution)/shard_map/ppermute | solution.py:40
  270.7 15.9 %collective-permute-start.85 = (bf16[384,896]{1,0:T(8,128)(2,1)S(1)}, bf16[384,896]{1,0:T(8,128)(2,1)S(1)}, u32[]{:S(2)}, u32[]{:S(2)}) collective-permute-start(bf16[384,896]{1,0:T(8,128)(2,1)S(1)} %get-tuple-element.223.refs_4_), channel_id=1, source_target_pairs={{0,4},{4,0},{8,12},{12,8},{1,5},{5,1},{9,13},{13,9},{2,6},{6,2},{1... | collective-permute-start | bytes 2064392 | tf_op jit(solution)/shard_map/ppermute | solution.py:56
  271.5 13.4 %collective-permute-start.86 = (bf16[384,768]{1,0:T(8,128)(2,1)S(1)}, bf16[384,768]{1,0:T(8,128)(2,1)S(1)}, u32[]{:S(2)}, u32[]{:S(2)}) collective-permute-start(bf16[384,768]{1,0:T(8,128)(2,1)S(1)} %get-tuple-element.225), channel_id=1, source_target_pairs={{0,8},{4,12},{8,0},{12,4},{1,9},{5,13},{9,1},{13,5},{2,10},{6,14},... | collective-permute-start | bytes 1769480 | tf_op jit(solution)/shard_map/ppermute | solution.py:56
  286.9 11.6 %collective-permute-start.87 = (bf16[192,896]{1,0:T(8,128)(2,1)S(1)}, bf16[192,896]{1,0:T(8,128)(2,1)S(1)}, u32[]{:S(2)}, u32[]{:S(2)}) collective-permute-start(bf16[192,896]{1,0:T(8,128)(2,1)S(1)} %get-tuple-element.228), channel_id=1, source_target_pairs={{0,8},{4,12},{8,0},{12,4},{1,9},{5,13},{9,1},{13,5},{2,10},{6,14},... | collective-permute-start | bytes 1032200 | tf_op jit(solution)/shard_map/ppermute | solution.py:56
  290.4 12.1 %collective-permute-start.93 = (bf16[48,1536]{1,0:T(8,128)(2,1)S(1)}, bf16[48,1536]{1,0:T(8,128)(2,1)S(1)}, u32[]{:S(2)}, u32[]{:S(2)}) collective-permute-start(bf16[48,1536]{1,0:T(8,128)(2,1)S(1)} %get-tuple-element.236), channel_id=1, source_target_pairs={{0,1},{1,0},{2,3},{3,2},{4,5},{5,4},{6,7},{7,6},{8,9},{9,8},{10,11... | collective-permute-start | bytes 442376 | tf_op jit(solution)/shard_map/ppermute | solution.py:56
  291.1 13.4 %collective-permute-start.94 = (bf16[48,1536]{1,0:T(8,128)(2,1)S(1)}, bf16[48,1536]{1,0:T(8,128)(2,1)S(1)}, u32[]{:S(2)}, u32[]{:S(2)}) collective-permute-start(bf16[48,1536]{1,0:T(8,128)(2,1)S(1)} %get-tuple-element.237), channel_id=1, source_target_pairs={{0,2},{1,3},{2,0},{3,1},{4,6},{5,7},{6,4},{7,5},{8,10},{9,11},{10,... | collective-permute-start | bytes 442376 | tf_op jit(solution)/shard_map/ppermute | solution.py:56
  292.0 15.0 %collective-permute-start.95 = (bf16[48,1536]{1,0:T(8,128)(2,1)S(1)}, bf16[48,1536]{1,0:T(8,128)(2,1)S(1)}, u32[]{:S(2)}, u32[]{:S(2)}) collective-permute-start(bf16[48,1536]{1,0:T(8,128)(2,1)S(1)} %get-tuple-element.238), channel_id=1, source_target_pairs={{0,3},{1,2},{2,1},{3,0},{4,7},{5,6},{6,5},{7,4},{8,11},{9,10},{10,... | collective-permute-start | bytes 442376 | tf_op jit(solution)/shard_map/ppermute | solution.py:56
  301.3 15.3 %collective-permute-start.91 = (bf16[48,1664]{1,0:T(8,128)(2,1)S(1)}, bf16[48,1664]{1,0:T(8,128)(2,1)S(1)}, u32[]{:S(2)}, u32[]{:S(2)}) collective-permute-start(bf16[48,1664]{1,0:T(8,128)(2,1)S(1)} %get-tuple-element.234), channel_id=1, source_target_pairs={{0,2},{1,3},{2,0},{3,1},{4,6},{5,7},{6,4},{7,5},{8,10},{9,11},{10,... | collective-permute-start | bytes 479240 | tf_op jit(solution)/shard_map/ppermute | solution.py:56
  302.5 14.2 %collective-permute-start.92 = (bf16[48,1664]{1,0:T(8,128)(2,1)S(1)}, bf16[48,1664]{1,0:T(8,128)(2,1)S(1)}, u32[]{:S(2)}, u32[]{:S(2)}) collective-permute-start(bf16[48,1664]{1,0:T(8,128)(2,1)S(1)} %get-tuple-element.235), channel_id=1, source_target_pairs={{0,3},{1,2},{2,1},{3,0},{4,7},{5,6},{6,5},{7,4},{8,11},{9,10},{10,... | collective-permute-start | bytes 479240 | tf_op jit(solution)/shard_map/ppermute | solution.py:56
  304.6 15.9 %collective-permute-start.79 = (bf16[64,768]{1,0:T(8,128)(2,1)S(1)}, bf16[64,768]{1,0:T(8,128)(2,1)S(1)}, u32[]{:S(2)}, u32[]{:S(2)}) collective-permute-start(bf16[64,768]{1,0:T(8,128)(2,1)S(1)} %broadcast_select_fusion.1), channel_id=1, source_target_pairs={{0,16},{16,0},{1,17},{17,1},{2,18},{18,2},{3,19},{19,3},{4,20},{20... | collective-permute-start | bytes 294920 | tf_op jit(solution)/shard_map/ppermute | solution.py:40
  (59 other events, 382.7 us)
